TPU v7x, 256 devices: a whole 4x4x8 slice. The times are simulated.
256 devices in a mesh: dom: 64 (over x, z, core), rep: 4 (over y).
Axes of the slice: x: 4, y: 4, z: 8, core: 2. Of those that a mesh axis runs over, the one named last changes fastest.
Arguments:
- features: bfloat16 [196608, 512], P('dom', 'rep')
- send_rows: int32 [4096, 192], P('dom'), may hold values from 0 to 3071
- neighbours: int32 [196608, 10], P('dom'), may hold values from 0 to 15359
- w_self1: bfloat16 [512, 512], P(None, 'rep'), may hold values from -0.25 to 0.25
- w_neigh1: bfloat16 [512, 512], P(None, 'rep'), may hold values from -0.25 to 0.25
- w_self2: bfloat16 [512, 512], P(None, 'rep'), may hold values from -0.25 to 0.25
- w_neigh2: bfloat16 [512, 512], P(None, 'rep'), may hold values from -0.25 to 0.25
- queries: bfloat16 [16384, 512], P('dom', 'rep'), may hold values from -0.25 to 0.25
- owners: int32 [16384, 4], P('dom'), may hold values from 0 to 63, all different within a row; in each aligned block of 256 rows (0 to 255, 256 to 511, ...) at most 32 rows name the same one
- slate: int32 [16384, 4, 8], P('dom'), may hold values from 0 to 3071
Outputs:
- node_embed: bfloat16 [196608, 512], P('dom', 'rep')
- scores: float32 [16384, 32], P('dom')
Inputs may be any that keep to these rules, and one draw needn't show every extreme that they name: `neighbours`: indices below 3072 are the partition's own nodes; index 3072 + s * 192 + r is row r of what partition s sends to this one. `owners`: each row names 4 different partitions; among the rows of one partition no partition is named by more than 32 rows, and that bound is reached.
All inputs are finite; a program needn't handle non-finite values.
Results may differ from a plain program's by a relative error of at most 0.0053.
Values may be sent and summed in bfloat16 or wider, within the bound.
A program may use at most 64 MiB of HBM per device.

v0:
```python
import jax
import jax.numpy as jnp
from jax import lax
from jax.sharding import PartitionSpec as P

F = 512
K = 10
TOPQ = 4
S = 8


def sage_layer(h_rows, send_rows, neighbours, w_self, w_neigh, active):
    width = h_rows.shape[1]
    outgoing = h_rows[send_rows]
    incoming = lax.all_to_all(outgoing, "dom", split_axis=0, concat_axis=0, tiled=True)
    table = jnp.concatenate([h_rows, incoming.reshape(-1, width)], axis=0)
    summed = jnp.zeros((h_rows.shape[0], width), jnp.float32)
    for column in range(neighbours.shape[1]):
        summed = summed + table[neighbours[:, column]].astype(jnp.float32)
    agg = (summed / K).astype(jnp.bfloat16)
    total = jnp.dot(
        lax.all_gather(h_rows, "rep", axis=1, tiled=True),
        w_self,
        preferred_element_type=jnp.float32,
    )
    z = total + jnp.dot(
        lax.all_gather(agg, "rep", axis=1, tiled=True), w_neigh, preferred_element_type=jnp.float32
    )
    if active:
        z = jax.nn.relu(z)
    squares = lax.psum(jnp.sum(z * z, axis=1), "rep")
    scale = lax.rsqrt(squares / F + 1e-06)
    return (z * scale[:, None]).astype(jnp.bfloat16)


def body(
    features, send_rows, neighbours, w_self1, w_neigh1, w_self2, w_neigh2, queries, owners, slate
):
    hidden_one = sage_layer(features, send_rows, neighbours, w_self1, w_neigh1, True)
    node_embed = sage_layer(hidden_one, send_rows, neighbours, w_self2, w_neigh2, False)
    ndom = lax.axis_size("dom")
    sessions = queries.shape[0]
    width = queries.shape[1]
    capacity = min(sessions, 2 * sessions * TOPQ // ndom)
    flat_owner = owners.reshape(-1)
    onehot = (flat_owner[:, None] == jnp.arange(ndom, dtype=jnp.int32)[None, :]).astype(jnp.int32)
    before = jnp.cumsum(onehot, axis=0) - onehot
    position = jnp.sum(before * onehot, axis=1)
    slot_index = flat_owner * capacity + position
    flat_slate = slate.reshape(sessions * TOPQ, S)
    send_lists = jnp.zeros((ndom * capacity, S), jnp.int32).at[slot_index].set(flat_slate)
    send_lists = send_lists.reshape(ndom, capacity, S)
    query_copies = jnp.repeat(queries, TOPQ, axis=0)
    got_lists = lax.all_to_all(send_lists, "dom", split_axis=0, concat_axis=0, tiled=True)
    items = node_embed[got_lists.reshape(-1)].reshape(ndom, capacity, S, width)
    fetched = lax.all_to_all(items, "dom", split_axis=0, concat_axis=0, tiled=True)
    picked = fetched.reshape(ndom * capacity, S, width)[slot_index]
    partial_value = jnp.einsum(
        "qf,qsf->qs", query_copies, picked, preferred_element_type=jnp.float32
    )
    partial_value = partial_value.reshape(sessions, TOPQ * S)
    scores = lax.psum(partial_value, "rep")
    return (node_embed, scores)


def solution(mesh):
    placed = (
        P("dom", "rep"),
        P("dom", None),
        P("dom", None),
        P(None, "rep"),
        P(None, "rep"),
        P(None, "rep"),
        P(None, "rep"),
        P("dom", "rep"),
        P("dom", None),
        P("dom", None, None),
    )
    return jax.shard_map(
        body,
        mesh=mesh,
        in_specs=placed,
        out_specs=(P("dom", "rep"), P("dom", None)),
        check_vma=False,
    )
```

profile of v0, /device:TPU:1, one launch (start us, length us, event | category | flops | bytes accessed | tf_op | source)
XLA Modules:
  0.0 849.1 jit_solution(5970493303241721797)
XLA Ops:
  8.2 42.7 %gather_fusion = bf16[12288,128]{1,0:T(8,128)(2,1)} fusion(bf16[3072,128]{1,0:T(8,128)(2,1)} %param.10, s32[12288]{0:T(1024)S(1)} %broadcast_clamp_fusion.1), kind=kCustom, calls=%fused_computation | custom fusion | bytes 6340608 | tf_op jit(solution)/shard_map/gather | solution.py:14
  50.9 13.3 %all-to-all-start = ((bf16[64,192,128]{2,1,0:T(8,128)(2,1)}), bf16[64,192,128]{2,1,0:T(8,128)(2,1)}, u32[]{:S(2)}, u32[]{:S(2)}) async-start(bf16[64,192,128]{2,1,0:T(8,128)(2,1)} %bitcast.56), calls=%async_computation | async-start | bytes 6291456 | tf_op jit(solution)/shard_map/all_to_all | solution.py:15
  65.3 72.3 %all-to-all-done = bf16[64,192,128]{2,1,0:T(8,128)(2,1)} async-done(((bf16[64,192,128]{2,1,0:T(8,128)(2,1)}), bf16[64,192,128]{2,1,0:T(8,128)(2,1)}, u32[]{:S(2)}, u32[]{:S(2)}) %all-to-all-start) | async-done | bytes 3145760 | tf_op jit(solution)/shard_map/all_to_all | solution.py:15
  137.6 5.6 pad_maximum_fusion
  143.2 10.9 %gather_fusion.1 = bf16[3072,128]{1,0:T(8,128)(2,1)S(1)} fusion(bf16[15360,128]{1,0:T(8,128)(2,1)} %pad_maximum_fusion, s32[3072]{0:T(1024)S(1)} %broadcast_clamp_fusion.11), kind=kCustom, calls=%fused_computation.1 | custom fusion | bytes 1585152 | tf_op jit(solution)/shard_map/gather | solution.py:19
  154.2 10.9 %gather_fusion.10 = bf16[3072,128]{1,0:T(8,128)(2,1)S(1)} fusion(bf16[15360,128]{1,0:T(8,128)(2,1)} %pad_maximum_fusion, s32[3072]{0:T(1024)S(1)} %broadcast_clamp_fusion.2), kind=kCustom, calls=%fused_computation.10 | custom fusion | bytes 1585152 | tf_op jit(solution)/shard_map/gather | solution.py:19
  165.1 10.9 %gather_fusion.2 = bf16[3072,128]{1,0:T(8,128)(2,1)S(1)} fusion(bf16[15360,128]{1,0:T(8,128)(2,1)} %pad_maximum_fusion, s32[3072]{0:T(1024)S(1)} %broadcast_clamp_fusion.10), kind=kCustom, calls=%fused_computation.2 | custom fusion | bytes 1585152 | tf_op jit(solution)/shard_map/gather | solution.py:19
  176.0 10.9 %gather_fusion.3 = bf16[3072,128]{1,0:T(8,128)(2,1)S(1)} fusion(bf16[15360,128]{1,0:T(8,128)(2,1)} %pad_maximum_fusion, s32[3072]{0:T(1024)S(1)} %broadcast_clamp_fusion.9), kind=kCustom, calls=%fused_computation.3 | custom fusion | bytes 1585152 | tf_op jit(solution)/shard_map/gather | solution.py:19
  187.0 13.5 %gather_fusion.4 = bf16[3072,128]{1,0:T(8,128)(2,1)} fusion(bf16[15360,128]{1,0:T(8,128)(2,1)} %pad_maximum_fusion, s32[3072]{0:T(1024)S(1)} %broadcast_clamp_fusion.8), kind=kCustom, calls=%fused_computation.4 | custom fusion | bytes 1585152 | tf_op jit(solution)/shard_map/gather | solution.py:19
  200.5 13.5 %gather_fusion.5 = bf16[3072,128]{1,0:T(8,128)(2,1)} fusion(bf16[15360,128]{1,0:T(8,128)(2,1)} %pad_maximum_fusion, s32[3072]{0:T(1024)S(1)} %broadcast_clamp_fusion.7), kind=kCustom, calls=%fused_computation.5 | custom fusion | bytes 1585152 | tf_op jit(solution)/shard_map/gather | solution.py:19
  214.1 13.5 %gather_fusion.6 = bf16[3072,128]{1,0:T(8,128)(2,1)} fusion(bf16[15360,128]{1,0:T(8,128)(2,1)} %pad_maximum_fusion, s32[3072]{0:T(1024)S(1)} %broadcast_clamp_fusion.6), kind=kCustom, calls=%fused_computation.6 | custom fusion | bytes 1585152 | tf_op jit(solution)/shard_map/gather | solution.py:19
  227.6 13.6 %gather_fusion.7 = bf16[3072,128]{1,0:T(8,128)(2,1)} fusion(bf16[15360,128]{1,0:T(8,128)(2,1)} %pad_maximum_fusion, s32[3072]{0:T(1024)S(1)} %broadcast_clamp_fusion.5), kind=kCustom, calls=%fused_computation.7 | custom fusion | bytes 1585152 | tf_op jit(solution)/shard_map/gather | solution.py:19
  241.2 13.5 %gather_fusion.8 = bf16[3072,128]{1,0:T(8,128)(2,1)} fusion(bf16[15360,128]{1,0:T(8,128)(2,1)} %pad_maximum_fusion, s32[3072]{0:T(1024)S(1)} %broadcast_clamp_fusion.4), kind=kCustom, calls=%fused_computation.8 | custom fusion | bytes 1585152 | tf_op jit(solution)/shard_map/gather | solution.py:19
  254.7 13.7 %gather_fusion.9 = bf16[3072,128]{1,0:T(8,128)(2,1)} fusion(bf16[15360,128]{1,0:T(8,128)(2,1)} %pad_maximum_fusion, s32[3072]{0:T(1024)S(1)} %broadcast_clamp_fusion.3), kind=kCustom, calls=%fused_computation.9 | custom fusion | bytes 1585152 | tf_op jit(solution)/shard_map/gather | solution.py:19
  268.4 4.3 multiply_convert_fusion.3
  272.7 2.9 fusion.9
  275.6 39.1 %all-gather.7.cloned.1.call-done = bf16[3072,512]{1,0:T(8,128)(2,1)} async-done(((bf16[3072,128]{1,0:T(8,128)(2,1)}), bf16[3072,512]{1,0:T(8,128)(2,1)}) %all-gather.7.cloned.1.call-update) | async-done | bytes 3145744 | tf_op jit(solution)/shard_map/all_gather | solution.py:27
  314.7 2.9 multiply_reduce_fusion.1
  317.6 12.5 %psum.21 = f32[3072]{0:T(1024)S(1)} all-reduce(f32[3072]{0:T(1024)S(1)} %get-tuple-element.22), channel_id=1, replica_groups=mesh['dom'=64,'rep'=4] {'rep'}, use_global_device_ids=true, to_apply=%region_1.2 | all-reduce | flops 3072 | bytes 24576 | tf_op jit(solution)/shard_map/psum | solution.py:31
  330.6 43.3 %gather_fusion.11 = bf16[12288,128]{1,0:T(8,128)(2,1)} fusion(bf16[3072,128]{1,0:T(8,128)(2,1)S(1)} %multiply_convert_fusion.2, s32[12288]{0:T(1024)S(1)} %broadcast_clamp_fusion.1), kind=kCustom, calls=%fused_computation.11 | custom fusion | bytes 6340608 | tf_op jit(solution)/shard_map/gather | solution.py:14
  373.9 15.5 %all-to-all-start.1 = ((bf16[64,192,128]{2,1,0:T(8,128)(2,1)}), bf16[64,192,128]{2,1,0:T(8,128)(2,1)}, u32[]{:S(2)}, u32[]{:S(2)}) async-start(bf16[64,192,128]{2,1,0:T(8,128)(2,1)} %bitcast.57), calls=%async_computation.1 | async-start | bytes 6291456 | tf_op jit(solution)/shard_map/all_to_all | solution.py:15
  390.6 18.0 %reduce-window.6 = s32[64,8,128]{2,1,0:T(8,128)S(1)} reduce-window(s32[64,8,128]{2,1,0:T(8,128)S(1)} %fusion.8, s32[]{:T(128)} %constant.9.clone.1), window={size=1x1x128 pad=0_0x0_0x127_0}, to_apply=%region_4.5 | reduce-window | flops 8323072 | bytes 524292 | tf_op jit(solution)/shard_map/reduce-window
  409.3 1.0 copy.49
  410.5 52.3 %all-to-all-done.1 = bf16[64,192,128]{2,1,0:T(8,128)(2,1)} async-done(((bf16[64,192,128]{2,1,0:T(8,128)(2,1)}), bf16[64,192,128]{2,1,0:T(8,128)(2,1)}, u32[]{:S(2)}, u32[]{:S(2)}) %all-to-all-start.1) | async-done | bytes 3145760 | tf_op jit(solution)/shard_map/all_to_all | solution.py:15
  462.8 5.6 pad_maximum_fusion.1
  468.4 10.9 %gather_fusion.12 = bf16[3072,128]{1,0:T(8,128)(2,1)S(1)} fusion(bf16[15360,128]{1,0:T(8,128)(2,1)} %pad_maximum_fusion.1, s32[3072]{0:T(1024)S(1)} %broadcast_clamp_fusion.11), kind=kCustom, calls=%fused_computation.12 | custom fusion | bytes 1585152 | tf_op jit(solution)/shard_map/gather | solution.py:19
  479.4 10.9 %gather_fusion.13 = bf16[3072,128]{1,0:T(8,128)(2,1)S(1)} fusion(bf16[15360,128]{1,0:T(8,128)(2,1)} %pad_maximum_fusion.1, s32[3072]{0:T(1024)S(1)} %broadcast_clamp_fusion.10), kind=kCustom, calls=%fused_computation.13 | custom fusion | bytes 1585152 | tf_op jit(solution)/shard_map/gather | solution.py:19
  490.3 10.9 %gather_fusion.14 = bf16[3072,128]{1,0:T(8,128)(2,1)S(1)} fusion(bf16[15360,128]{1,0:T(8,128)(2,1)} %pad_maximum_fusion.1, s32[3072]{0:T(1024)S(1)} %broadcast_clamp_fusion.9), kind=kCustom, calls=%fused_computation.14 | custom fusion | bytes 1585152 | tf_op jit(solution)/shard_map/gather | solution.py:19
  501.3 10.9 %gather_fusion.15 = bf16[3072,128]{1,0:T(8,128)(2,1)S(1)} fusion(bf16[15360,128]{1,0:T(8,128)(2,1)} %pad_maximum_fusion.1, s32[3072]{0:T(1024)S(1)} %broadcast_clamp_fusion.8), kind=kCustom, calls=%fused_computation.15 | custom fusion | bytes 1585152 | tf_op jit(solution)/shard_map/gather | solution.py:19
  512.2 13.5 %gather_fusion.16 = bf16[3072,128]{1,0:T(8,128)(2,1)} fusion(bf16[15360,128]{1,0:T(8,128)(2,1)} %pad_maximum_fusion.1, s32[3072]{0:T(1024)S(1)} %broadcast_clamp_fusion.7), kind=kCustom, calls=%fused_computation.16 | custom fusion | bytes 1585152 | tf_op jit(solution)/shard_map/gather | solution.py:19
  525.7 13.6 %gather_fusion.17 = bf16[3072,128]{1,0:T(8,128)(2,1)} fusion(bf16[15360,128]{1,0:T(8,128)(2,1)} %pad_maximum_fusion.1, s32[3072]{0:T(1024)S(1)} %broadcast_clamp_fusion.6), kind=kCustom, calls=%fused_computation.17 | custom fusion | bytes 1585152 | tf_op jit(solution)/shard_map/gather | solution.py:19
  539.3 13.6 %gather_fusion.18 = bf16[3072,128]{1,0:T(8,128)(2,1)} fusion(bf16[15360,128]{1,0:T(8,128)(2,1)} %pad_maximum_fusion.1, s32[3072]{0:T(1024)S(1)} %broadcast_clamp_fusion.5), kind=kCustom, calls=%fused_computation.18 | custom fusion | bytes 1585152 | tf_op jit(solution)/shard_map/gather | solution.py:19
  552.9 13.6 %gather_fusion.19 = bf16[3072,128]{1,0:T(8,128)(2,1)} fusion(bf16[15360,128]{1,0:T(8,128)(2,1)} %pad_maximum_fusion.1, s32[3072]{0:T(1024)S(1)} %copy-done.10), kind=kCustom, calls=%fused_computation.19 | custom fusion | bytes 1585152 | tf_op jit(solution)/shard_map/gather | solution.py:19
  566.4 13.5 %gather_fusion.20 = bf16[3072,128]{1,0:T(8,128)(2,1)} fusion(bf16[15360,128]{1,0:T(8,128)(2,1)} %pad_maximum_fusion.1, s32[3072]{0:T(1024)S(1)} %copy-done.12), kind=kCustom, calls=%fused_computation.20 | custom fusion | bytes 1585152 | tf_op jit(solution)/shard_map/gather | solution.py:19
  580.0 13.5 %gather_fusion.21 = bf16[3072,128]{1,0:T(8,128)(2,1)} fusion(bf16[15360,128]{1,0:T(8,128)(2,1)} %pad_maximum_fusion.1, s32[3072]{0:T(1024)S(1)} %broadcast_clamp_fusion.2), kind=kCustom, calls=%fused_computation.21 | custom fusion | bytes 1585152 | tf_op jit(solution)/shard_map/gather | solution.py:19
  593.5 4.3 multiply_convert_fusion.1
  597.8 4.0 scatter_custom_fusion
  602.3 15.7 %all_to_all.20 = s32[64,1,256]{2,1,0:T(1,128)S(1)} all-to-all(s32[64,1,256]{2,1,0:T(1,128)S(1)} %reshape.325), channel_id=1, replica_groups=mesh['dom'=64,'rep'=4] {'dom'}, dimensions={0} | all-to-all | bytes 131072 | tf_op jit(solution)/shard_map/all_to_all | solution.py:54
  620.4 3.1 fusion.10
  623.6 13.8 %all-gather.11.cloned.1.call-done = bf16[3072,512]{1,0:T(8,128)(2,1)} async-done(((bf16[3072,128]{1,0:T(8,128)(2,1)}), bf16[3072,512]{1,0:T(8,128)(2,1)}) %all-gather.11.cloned.1.call-update) | async-done | bytes 3145744 | tf_op jit(solution)/shard_map/all_gather | solution.py:27
  637.4 3.1 multiply_reduce_fusion
  640.5 12.5 %psum.22 = f32[3072]{0:T(1024)S(1)} all-reduce(f32[3072]{0:T(1024)S(1)} %get-tuple-element.24), channel_id=1, replica_groups=mesh['dom'=64,'rep'=4] {'rep'}, use_global_device_ids=true, to_apply=%region_3.4 | all-reduce | flops 3072 | bytes 24576 | tf_op jit(solution)/shard_map/psum | solution.py:31
  653.5 57.4 %gather_fusion.22 = bf16[16384,128]{1,0:T(8,128)(2,1)} fusion(bf16[3072,128]{1,0:T(8,128)(2,1)S(1)} %copy.54, s32[16384]{0:T(1024)S(1)} %broadcast_clamp_fusion), kind=kCustom, calls=%fused_computation.22 | custom fusion | bytes 8454144 | tf_op jit(solution)/shard_map/gather | solution.py:55
  710.9 15.4 %all-to-all-start.3 = ((bf16[64,32,8,128]{3,2,1,0:T(8,128)(2,1)}), bf16[64,32,8,128]{3,2,1,0:T(8,128)(2,1)}, u32[]{:S(2)}, u32[]{:S(2)}) async-start(bf16[64,32,8,128]{3,2,1,0:T(8,128)(2,1)} %bitcast.55), calls=%async_computation.3 | async-start | bytes 8388608 | tf_op jit(solution)/shard_map/all_to_all | solution.py:56
  726.3 95.9 %all-to-all-done.3 = bf16[64,32,8,128]{3,2,1,0:T(8,128)(2,1)} async-done(((bf16[64,32,8,128]{3,2,1,0:T(8,128)(2,1)}), bf16[64,32,8,128]{3,2,1,0:T(8,128)(2,1)}, u32[]{:S(2)}, u32[]{:S(2)}) %all-to-all-start.3) | async-done | bytes 4194336 | tf_op jit(solution)/shard_map/all_to_all | solution.py:56
  822.2 5.6 gather_fusion.23
  827.8 1.2 fusion.3
  829.2 12.6 %psum.23 = f32[256,32]{1,0:T(8,128)S(1)} all-reduce(f32[256,32]{1,0:T(8,128)S(1)} %reshape.116), channel_id=1, replica_groups=mesh['dom'=64,'rep'=4] {'rep'}, use_global_device_ids=true, to_apply=%region_8.9 | all-reduce | flops 8192 | bytes 65536 | tf_op jit(solution)/shard_map/psum | solution.py:62
  (91 shorter events, 8.9 us)
Async XLA Ops:
  7.2 307.5 %copy-start = (bf16[512,128]{1,0:T(8,128)(2,1)S(1)}, bf16[512,128]{1,0:T(8,128)(2,1)}, u32[]{:S(2)}) copy-start(bf16[512,128]{1,0:T(8,128)(2,1)} %param.14) | copy-start | bytes 393220
  50.9 14.1 %copy-start.13 = (s32[3072,10]{0,1:T(8,128)S(1)}, s32[3072,10]{0,1:T(8,128)}, u32[]{:S(2)}) copy-start(s32[3072,10]{0,1:T(8,128)} %param.12) | copy-start | bytes 368644
  50.9 86.7 %copy-start.5 = (bf16[3072,128]{1,0:T(8,128)(2,1)S(1)}, bf16[3072,128]{1,0:T(8,128)(2,1)}, u32[]{:S(2)}) copy-start(bf16[3072,128]{1,0:T(8,128)(2,1)} %param.10) | copy-start | bytes 2359300
  50.9 86.7 %all-to-all-start = ((bf16[64,192,128]{2,1,0:T(8,128)(2,1)}), bf16[64,192,128]{2,1,0:T(8,128)(2,1)}, u32[]{:S(2)}, u32[]{:S(2)}) async-start(bf16[64,192,128]{2,1,0:T(8,128)(2,1)} %bitcast.56), calls=%async_computation | async-start | bytes 6291456 | tf_op jit(solution)/shard_map/all_to_all | solution.py:15
  64.2 208.5 %all-gather.5.cloned.1.call-start = ((), (), s32[]{:S(2)}) async-start(), calls=%async_computation.4 | async-start | bytes 3932160 | tf_op jit(solution)/shard_map/all_gather | solution.py:22
  64.9 249.8 %all-gather.7.cloned.1.call-start = ((), (), s32[]{:S(2)}) async-start(), calls=%async_computation.5 | async-start | bytes 3932160 | tf_op jit(solution)/shard_map/all_gather | solution.py:27
  65.2 175.9 %copy-start.9 = (s32[3072]{0:T(1024)}, s32[3072]{0:T(1024)S(1)}, u32[]{:S(2)}) copy-start(s32[3072]{0:T(1024)S(1)} %broadcast_clamp_fusion.4) | copy-start | bytes 36868
  65.3 189.4 %copy-start.11 = (s32[3072]{0:T(1024)}, s32[3072]{0:T(1024)S(1)}, u32[]{:S(2)}) copy-start(s32[3072]{0:T(1024)S(1)} %broadcast_clamp_fusion.3) | copy-start | bytes 36868
  268.4 4.4 copy-start.6
  330.6 43.3 %copy-start.3 = (bf16[3072,128]{1,0:T(8,128)(2,1)}, bf16[3072,128]{1,0:T(8,128)(2,1)S(1)}, u32[]{:S(2)}) copy-start(bf16[3072,128]{1,0:T(8,128)(2,1)S(1)} %multiply_convert_fusion.2) | copy-start | bytes 2359300
  373.9 16.3 %copy-start.16 = (s32[256,4]{0,1:T(4,128)S(1)}, s32[256,4]{0,1:T(4,128)}, u32[]{:S(2)}) copy-start(s32[256,4]{0,1:T(4,128)} %param.18) | copy-start | bytes 12292
  373.9 88.9 %all-to-all-start.1 = ((bf16[64,192,128]{2,1,0:T(8,128)(2,1)}), bf16[64,192,128]{2,1,0:T(8,128)(2,1)}, u32[]{:S(2)}, u32[]{:S(2)}) async-start(bf16[64,192,128]{2,1,0:T(8,128)(2,1)} %bitcast.57), calls=%async_computation.1 | async-start | bytes 6291456 | tf_op jit(solution)/shard_map/all_to_all | solution.py:15
  389.4 19.9 %copy-start.15 = (s32[256,4,8]{0,2,1:T(8,128)S(1)}, s32[256,4,8]{0,2,1:T(8,128)}, u32[]{:S(2)}) copy-start(s32[256,4,8]{0,2,1:T(8,128)} %param.19) | copy-start | bytes 98308
  389.4 73.4 %copy-start.4 = (bf16[3072,128]{1,0:T(8,128)(2,1)S(1)}, bf16[3072,128]{1,0:T(8,128)(2,1)}, u32[]{:S(2)}) copy-start(bf16[3072,128]{1,0:T(8,128)(2,1)} %copy-done.3) | copy-start | bytes 2359300
  389.4 231.0 %all-gather.9.cloned.1.call-start = ((), (), s32[]{:S(2)}) async-start(), calls=%async_computation.6 | async-start | bytes 3932160 | tf_op jit(solution)/shard_map/all_gather | solution.py:22
  390.1 247.3 %all-gather.11.cloned.1.call-start = ((), (), s32[]{:S(2)}) async-start(), calls=%async_computation.7 | async-start | bytes 3932160 | tf_op jit(solution)/shard_map/all_gather | solution.py:27
  539.3 13.6 %copy-start.10 = (s32[3072]{0:T(1024)S(1)}, s32[3072]{0:T(1024)}, u32[]{:S(2)}) copy-start(s32[3072]{0:T(1024)} %copy-done.9) | copy-start | bytes 36868
  552.9 13.6 %copy-start.12 = (s32[3072]{0:T(1024)S(1)}, s32[3072]{0:T(1024)}, u32[]{:S(2)}) copy-start(s32[3072]{0:T(1024)} %copy-done.11) | copy-start | bytes 36868
  602.1 18.3 %copy-start.7 = (bf16[512,128]{1,0:T(8,128)(2,1)S(1)}, bf16[512,128]{1,0:T(8,128)(2,1)}, u32[]{:S(2)}) copy-start(bf16[512,128]{1,0:T(8,128)(2,1)} %param.15) | copy-start | bytes 393220
  620.4 17.0 %copy-start.8 = (bf16[512,128]{1,0:T(8,128)(2,1)S(1)}, bf16[512,128]{1,0:T(8,128)(2,1)}, u32[]{:S(2)}) copy-start(bf16[512,128]{1,0:T(8,128)(2,1)} %param.16) | copy-start | bytes 393220
  653.5 57.4 %copy-start.2 = (bf16[3072,128]{1,0:T(8,128)(2,1)}, bf16[3072,128]{1,0:T(8,128)(2,1)S(1)}, u32[]{:S(2)}) copy-start(bf16[3072,128]{1,0:T(8,128)(2,1)S(1)} %copy.54) | copy-start | bytes 2359300
  710.9 111.3 %all-to-all-start.3 = ((bf16[64,32,8,128]{3,2,1,0:T(8,128)(2,1)}), bf16[64,32,8,128]{3,2,1,0:T(8,128)(2,1)}, u32[]{:S(2)}, u32[]{:S(2)}) async-start(bf16[64,32,8,128]{3,2,1,0:T(8,128)(2,1)} %bitcast.55), calls=%async_computation.3 | async-start | bytes 8388608 | tf_op jit(solution)/shard_map/all_to_all | solution.py:56
  822.2 5.6 copy-start.14
  827.8 14.7 %copy-start.1 = (bf16[512,128]{1,0:T(8,128)(2,1)S(1)}, bf16[512,128]{1,0:T(8,128)(2,1)}, u32[]{:S(2)}) copy-start(bf16[512,128]{1,0:T(8,128)(2,1)} %param.14) | copy-start | bytes 393220
Sparse Core Ops, SparseCore 0:
  66.8 46.0 all-gather.4
  272.8 41.8 all-gather.6
  392.6 43.7 all-gather.8
  597.9 39.4 all-gather.10
where the time goes:
time: 852 us; the launch traced here: 849 us
  local copies, waits for them, and re-layouts  408 us (48%)
  waiting for transfers between devices  275 us (32%)
  blocking collectives  53.2 us (6%)
  starting transfers between devices  44.3 us (5%)
  other arithmetic  40.7 us (5%)
  between operations  14.3 us (2%)
  matrix products  13.2 us (2%)
    gather x20, local copies, waits for them, and re-layouts, sage_layer(): summed = summed + table[neighbours[:, column]].astype(jnp.float32)  250 us
    all_to_all x2, waiting for transfers between devices, sage_layer(): lax.all_to_all(outgoing, 'dom', split_axis=0, concat_axis=0, tiled=True)  125 us
    all_to_all x1, waiting for transfers between devices, body(): lax.all_to_all(items, 'dom', split_axis=0, concat_axis=0, tiled=True)  95.9 us
    gather x2, local copies, waits for them, and re-layouts, sage_layer(): outgoing = h_rows[send_rows]  86 us
    gather x1, local copies, waits for them, and re-layouts, body(): items = node_embed[got_lists.reshape(-1)].reshape(ndom, capacity, S, width)  57.4 us
    all_gather x2, waiting for transfers between devices, sage_layer(): lax.all_gather(agg, 'rep', axis=1, tiled=True)  52.9 us
    all_to_all x2, starting transfers between devices, sage_layer(): lax.all_to_all(outgoing, 'dom', split_axis=0, concat_axis=0, tiled=True)  28.8 us
    psum x2, blocking collectives, sage_layer(): squares = lax.psum(jnp.sum(z * z, axis=1), 'rep')  25 us
  transfers between devices with their start and end apart: 7, of which 5 were waited for; matrix products, arithmetic and copies ran while one was open for 36% of the time, Pallas kernels for 0%

commit v1 on v0

v1 whole, which is shorter than its diff:
```python
import functools

import jax
import jax.numpy as jnp
from jax import lax
from jax.experimental import pallas as pl
from jax.experimental.pallas import tpu as pltpu
from jax.sharding import PartitionSpec as P

MESH = pl.DeviceIdType.MESH
VMEM = pltpu.VMEM
F32 = jnp.float32
BF16 = jnp.bfloat16
LANE = 128
EPS = 1e-06


def rep_barrier(me, nrep):
    barrier = pltpu.get_barrier_semaphore()
    for step in range(1, nrep):
        pl.semaphore_signal(
            barrier, inc=1, device_id={"rep": lax.rem(me + step, nrep)}, device_id_type=MESH
        )
    pl.semaphore_wait(barrier, nrep - 1)


def columns_of(which):
    return pl.ds(pl.multiple_of(which * LANE, LANE), LANE)


def rows_of(which, count):
    return pl.ds(pl.multiple_of(which * count, count), count)


def pick_rows(index_ref, start, table, stage, count, unroll):
    def some(block, carry):
        base = block * unroll
        for u in range(unroll):
            stage[pl.ds(base + u, 1), :] = table[pl.ds(index_ref[start + base + u], 1), :]
        return carry

    lax.fori_loop(0, count // unroll, some, 0)


def send_gather(index_ref, table, stage, out_ref, parts, unroll):
    count = stage.shape[0]

    def part(p, carry):
        pick_rows(index_ref, p * count, table, stage, count, unroll)
        out_ref[rows_of(p, count), :] = stage[...].astype(BF16)
        return carry

    lax.fori_loop(0, parts, part, 0)


def sum_rows(index_ref, start, table, stage, nodes, fan, unroll):
    def some(block, carry):
        base = block * unroll
        for u in range(unroll):
            terms = [
                table[pl.ds(index_ref[k * nodes + start + base + u], 1), :] for k in range(fan)
            ]
            while len(terms) > 1:
                pairs = [terms[i] + terms[i + 1] for i in range(0, len(terms) - 1, 2)]
                terms = pairs + terms[len(pairs) * 2 :]
            stage[pl.ds(base + u, 1), :] = terms[0]
        return carry

    lax.fori_loop(0, stage.shape[0] // unroll, some, 0)


def first_kernel(nrep, ndom, send_idx, own, out_rows, outgoing, table, stage, send, recv, local):
    me = lax.axis_index("rep")
    chunk = own.shape[0] // nrep
    rep_barrier(me, nrep)
    copies = []
    for step in range(nrep - 1):
        to = lax.rem(me + 1 + step, nrep)
        copy = pltpu.make_async_remote_copy(
            src_ref=own.at[rows_of(to, chunk), :],
            dst_ref=out_rows.at[:, columns_of(me)],
            send_sem=send.at[step],
            recv_sem=recv.at[step],
            device_id={"rep": to},
            device_id_type=MESH,
        )
        copy.start()
        copies.append(copy)
    mine = pltpu.make_async_copy(
        own.at[rows_of(me, chunk), :], out_rows.at[:, columns_of(me)], local.at[0]
    )
    mine.start()
    table[...] = own[...].astype(F32)
    send_gather(send_idx, table, stage, outgoing, ndom, 32)
    mine.wait()
    for copy in copies:
        copy.wait()


def layer_core(
    nrep, fan, active, neigh_idx, own, incoming, self_rows, weights,
    hid_rows, hid_cols, table, stage, chunks, agg_rows, send, recv, hsend, hrecv, local,
):
    me = lax.axis_index("rep")
    nodes = own.shape[0]
    chunk = nodes // nrep
    width = self_rows.shape[1]
    rep_barrier(me, nrep)
    table[pl.ds(0, nodes), :] = own[...].astype(F32)
    table[pl.ds(nodes, incoming.shape[0]), :] = incoming[...].astype(F32)
    copies = []
    for step in range(nrep):
        to = lax.rem(me + 1 + step, nrep)
        sum_rows(neigh_idx, to * chunk, table, stage, nodes, fan, 16)
        chunks[step] = (stage[...] / fan).astype(BF16)
        if step < nrep - 1:
            copy = pltpu.make_async_remote_copy(
                src_ref=chunks.at[step],
                dst_ref=agg_rows.at[:, columns_of(me)],
                send_sem=send.at[step],
                recv_sem=recv.at[step],
                device_id={"rep": to},
                device_id_type=MESH,
            )
        else:
            copy = pltpu.make_async_copy(
                chunks.at[step], agg_rows.at[:, columns_of(me)], local.at[0]
            )
        copy.start()
        copies.append(copy)
    for copy in copies:
        copy.wait()
    tiles = hsend.shape[0]
    tile = chunk // tiles
    back = []
    for t in range(tiles):
        rows = pl.ds(t * tile, tile)
        z = jnp.dot(self_rows[rows, :], weights[pl.ds(0, width), :], preferred_element_type=F32)
        z = z + jnp.dot(
            agg_rows[rows, :], weights[pl.ds(width, width), :], preferred_element_type=F32
        )
        if active:
            z = jnp.maximum(z, 0.0)
        mean = jnp.sum(z * z, axis=1, keepdims=True) / width
        hid_rows[rows, :] = (z * lax.rsqrt(mean + EPS)).astype(BF16)
        landing = pl.ds(pl.multiple_of(me * chunk + t * tile, tile), tile)
        for step in range(nrep - 1):
            to = lax.rem(me + 1 + step, nrep)
            copy = pltpu.make_async_remote_copy(
                src_ref=hid_rows.at[rows, columns_of(to)],
                dst_ref=hid_cols.at[landing, :],
                send_sem=hsend.at[t, step],
                recv_sem=hrecv.at[t, step],
                device_id={"rep": to},
                device_id_type=MESH,
            )
            copy.start()
            back.append(copy)
        copy = pltpu.make_async_copy(
            hid_rows.at[rows, columns_of(me)], hid_cols.at[landing, :], local.at[1 + t]
        )
        copy.start()
        back.append(copy)
    for copy in back:
        copy.wait()
    table[pl.ds(0, nodes), :] = hid_cols[...].astype(F32)


def middle_kernel(
    nrep, ndom, fan, neigh_idx, send_idx, own, incoming, self_rows, weights,
    hid_rows, hid_cols, outgoing, table, stage, pick, chunks, agg_rows, *sems,
):
    layer_core(
        nrep, fan, True, neigh_idx, own, incoming, self_rows, weights,
        hid_rows, hid_cols, table, stage, chunks, agg_rows, *sems,
    )
    send_gather(send_idx, table, pick, outgoing, ndom, 32)


def last_kernel(
    nrep, ndom, fan, neigh_idx, items, own, incoming, self_rows, weights, queries,
    hid_cols, scores, table, stage, pick, chunks, agg_rows, hid_rows, partial, psend, precv, *sems,
):
    me = lax.axis_index("rep")
    layer_core(
        nrep, fan, False, neigh_idx, own, incoming, self_rows, weights,
        hid_rows, hid_cols, table, stage, chunks, agg_rows, *sems,
    )
    count = pick.shape[0]
    slots = queries.shape[0] // ndom
    owns = lax.broadcasted_iota(jnp.int32, (slots, count), 0)
    slot = lax.rem(lax.broadcasted_iota(jnp.int32, (slots, count), 1), slots)

    def part(p, carry):
        pick_rows(items, p * count, table, pick, count, 32)
        products = lax.dot_general(
            queries[rows_of(p, slots), :],
            pick[...].astype(BF16),
            (((1,), (1,)), ((), ())),
            preferred_element_type=F32,
        )
        partial[me, pl.ds(p, 1), :] = jnp.sum(
            jnp.where(owns == slot, products, 0.0), axis=0, keepdims=True
        )
        return carry

    lax.fori_loop(0, ndom, part, 0)
    copies = []
    for step in range(nrep - 1):
        copy = pltpu.make_async_remote_copy(
            src_ref=partial.at[me],
            dst_ref=partial.at[me],
            send_sem=psend.at[step],
            recv_sem=precv.at[step],
            device_id={"rep": lax.rem(me + 1 + step, nrep)},
            device_id_type=MESH,
        )
        copy.start()
        copies.append(copy)
    for copy in copies:
        copy.wait()
    total = partial[0]
    for other in range(1, nrep):
        total = total + partial[other]
    scores[...] = total


def call(kernel, name, number, outs, scratch, smem, args):
    whole = pl.BlockSpec(memory_space=VMEM)
    return pl.pallas_call(
        kernel,
        out_shape=outs,
        in_specs=[pl.BlockSpec(memory_space=pltpu.SMEM)] * smem + [whole] * (len(args) - smem),
        out_specs=[whole] * len(outs),
        scratch_shapes=scratch,
        compiler_params=pltpu.CompilerParams(
            collective_id=number, has_side_effects=True, vmem_limit_bytes=44 * 1024 * 1024
        ),
        name=name,
    )(*args)


def body(
    features, send_rows, neighbours, w_self1, w_neigh1, w_self2, w_neigh2, queries, owners, slate
):
    ndom, nrep = lax.axis_size("dom"), lax.axis_size("rep")
    nodes, width = features.shape
    fan = neighbours.shape[1]
    per_pair = send_rows.shape[1]
    chunk = nodes // nrep
    full = width * nrep
    sessions, topq, nitems = slate.shape
    capacity = min(sessions, 2 * sessions * topq // ndom)
    entries, nslots = sessions * topq, ndom * capacity
    count = capacity * nitems
    tiles = 3
    dma = pltpu.SemaphoreType.DMA

    send_idx = send_rows.reshape(-1)
    neigh_idx = neighbours.T.reshape(-1)
    weights1 = lax.all_gather(jnp.concatenate([w_self1, w_neigh1], 0), "rep", axis=1, tiled=True)
    weights2 = lax.all_gather(jnp.concatenate([w_self2, w_neigh2], 0), "rep", axis=1, tiled=True)

    shape = jax.ShapeDtypeStruct
    x_rows, outgoing = call(
        functools.partial(first_kernel, nrep, ndom),
        "send_gather",
        1,
        [shape((chunk, full), BF16), shape((ndom * per_pair, width), BF16)],
        [
            VMEM((nodes, width), F32),
            VMEM((per_pair, width), F32),
            dma((nrep - 1,)),
            dma((nrep - 1,)),
            dma((1,)),
        ],
        1,
        [send_idx, features],
    )

    def exchange(rows):
        rows = rows.reshape(ndom, per_pair, width)
        rows = lax.all_to_all(rows, "dom", split_axis=0, concat_axis=0, tiled=True)
        return rows.reshape(ndom * per_pair, width)

    incoming = exchange(outgoing)

    owner_of = owners.T.reshape(entries)
    named = owner_of[:, None] == jnp.arange(ndom, dtype=jnp.int32)[None, :]
    order = jnp.arange(entries, dtype=jnp.int32)
    earlier = (order[:, None] > order[None, :]).astype(BF16)
    before = jnp.dot(earlier, named.astype(BF16), preferred_element_type=F32)
    position = jnp.sum(jnp.where(named, before, 0.0), axis=1).astype(jnp.int32)
    slot_index = owner_of * capacity + position
    place = (jnp.arange(nslots, dtype=jnp.int32)[:, None] == slot_index[None, :]).astype(BF16)
    slot_queries = jnp.dot(place, jnp.tile(queries, (topq, 1)), preferred_element_type=F32)
    slot_queries = slot_queries.astype(BF16).reshape(ndom, capacity, width)
    lists = slate.transpose(1, 0, 2).reshape(entries, nitems)
    digits = jnp.concatenate([lists // 64, lists % 64], axis=1).astype(BF16)
    slot_digits = jnp.dot(place, digits, preferred_element_type=F32).astype(BF16)
    slot_digits = slot_digits.reshape(ndom, capacity * 2 * nitems // width, width)
    sent = jnp.concatenate([slot_queries, slot_digits], axis=1)
    got = lax.all_to_all(sent, "dom", split_axis=0, concat_axis=0, tiled=True)
    got_queries = got[:, :capacity].reshape(nslots, width)
    got_digits = got[:, capacity:].reshape(ndom, capacity, 2, nitems).astype(jnp.int32)
    items = (got_digits[:, :, 0] * 64 + got_digits[:, :, 1]).transpose(0, 2, 1).reshape(-1)

    table = VMEM((nodes + ndom * per_pair, width), F32)
    stage = VMEM((chunk, width), F32)
    chunks = VMEM((nrep, chunk, width), BF16)
    agg_rows = VMEM((chunk, full), BF16)
    hid_rows = VMEM((chunk, full), BF16)
    sems = [
        dma((nrep - 1,)),
        dma((nrep - 1,)),
        dma((tiles, nrep - 1)),
        dma((tiles, nrep - 1)),
        dma((1 + tiles,)),
    ]
    h_rows, h_cols, outgoing = call(
        functools.partial(middle_kernel, nrep, ndom, fan),
        "layer_one",
        2,
        [
            shape((chunk, full), BF16),
            shape((nodes, width), BF16),
            shape((ndom * per_pair, width), BF16),
        ],
        [table, stage, VMEM((per_pair, width), F32), chunks, agg_rows] + sems,
        2,
        [neigh_idx, send_idx, features, incoming, x_rows, weights1],
    )
    incoming = exchange(outgoing)
    node_embed, slot_scores = call(
        functools.partial(last_kernel, nrep, ndom, fan),
        "layer_two",
        3,
        [shape((nodes, width), BF16), shape((ndom, count), F32)],
        [table, stage, VMEM((count, width), F32), chunks, agg_rows, hid_rows]
        + [VMEM((nrep, ndom, count), F32), dma((nrep - 1,)), dma((nrep - 1,))]
        + sems,
        2,
        [neigh_idx, items, h_cols, incoming, h_rows, weights2, got_queries],
    )
    fetched = lax.all_to_all(slot_scores, "dom", split_axis=0, concat_axis=0, tiled=True)
    fetched = fetched.reshape(ndom, nitems, capacity).transpose(0, 2, 1).reshape(nslots, nitems)
    scores = fetched[slot_index].reshape(topq, sessions, nitems)
    return (node_embed, scores.transpose(1, 0, 2).reshape(sessions, topq * nitems))


def solution(mesh):
    placed = (
        P("dom", "rep"),
        P("dom", None),
        P("dom", None),
        P(None, "rep"),
        P(None, "rep"),
        P(None, "rep"),
        P(None, "rep"),
        P("dom", "rep"),
        P("dom", None),
        P("dom", None, None),
    )
    return jax.shard_map(
        body,
        mesh=mesh,
        in_specs=placed,
        out_specs=(P("dom", "rep"), P("dom", None)),
        check_vma=False,
    )
```

time: 852 us -> 380 us (0.45)
  local copies, waits for them, and re-layouts: 408 us -> 31.2 us
  Pallas kernels: 0 us -> 147 us
  waiting for transfers between devices: 275 us -> 140 us
  blocking collectives: 53.2 us -> 0 us
  other arithmetic: 40.7 us -> 4.25 us
  matrix products: 13.2 us -> 3.6 us
    gather x24 -> x1, local copies, waits for them, and re-layouts: 399 us -> 2.82 us  [body(): scores = fetched[slot_index].reshape(topq, sessions, nitems)]
    pallas_call x0 -> x3, Pallas kernels: none -> 147 us  [call(): pl.pallas_call(kernel, out_shape=outs, in_specs=[pl.BlockSpec(memory_spac...]
    all_to_all x3 -> x4, waiting for transfers between devices: 220 us -> 118 us  [the longest x2 109 us: exchange(): rows = lax.all_to_all(rows, 'dom', split_axis=0, concat_axis=0, tiled=True)]
    psum x3 -> x0, blocking collectives: 37.6 us -> none  [the longest x2 25 us: sage_layer(): squares = lax.psum(jnp.sum(z * z, axis=1), 'rep')]
    all_gather x4 -> x2, waiting for transfers between devices: 53 us -> 21.2 us  [the longest x1 21.2 us: body(): lax.all_gather(jnp.concatenate([w_self2, w_neigh2], 0), 'rep', axis=1, ti...]
    another operation x3 -> x1, other arithmetic: 18.2 us -> 0.04 us
    all_to_all x1 -> x0, blocking collectives: 15.7 us -> none  [body(): lax.all_to_all(send_lists, 'dom', split_axis=0, concat_axis=0, tiled=True)]
    unnamed x40 -> x44, local copies, waits for them, and re-layouts: 2.55 us -> 16.2 us
  transfers between devices with their start and end apart: 7 -> 6, of which waited for: 5 -> 4; matrix products, arithmetic and copies ran while one was open for 36% -> 5% of each run, Pallas kernels for 0% -> 15%
where the time goes in v1:
time: 380 us; the launch traced here: 379 us
  Pallas kernels  147 us (39%)
  waiting for transfers between devices  140 us (37%)
  starting transfers between devices  38.1 us (10%)
  local copies, waits for them, and re-layouts  31.2 us (8%)
  between operations  14.4 us (4%)
  other arithmetic  4.25 us (1%)
    pallas_call x3, Pallas kernels, call(): pl.pallas_call(kernel, out_shape=outs, in_specs=[pl.BlockSpec(memory_spac...  147 us
    all_to_all x2, waiting for transfers between devices, exchange(): rows = lax.all_to_all(rows, 'dom', split_axis=0, concat_axis=0, tiled=True)  109 us
    all_to_all x2, starting transfers between devices, exchange(): rows = lax.all_to_all(rows, 'dom', split_axis=0, concat_axis=0, tiled=True)  24.3 us
    all_gather x1, waiting for transfers between devices, body(): lax.all_gather(jnp.concatenate([w_self2, w_neigh2], 0), 'rep', axis=1, ti...  21.2 us
    unnamed x44, local copies, waits for them, and re-layouts  16.2 us
    all_to_all x1, waiting for transfers between devices, body(): lax.all_to_all(slot_scores, 'dom', split_axis=0, concat_axis=0, tiled=True)  9.77 us
  transfers between devices with their start and end apart: 6, of which 4 were waited for; matrix products, arithmetic and copies ran while one was open for 5% of the time, Pallas kernels for 15%

profile of v1, /device:TPU:1, one launch (start us, length us, event | category | flops | bytes accessed | tf_op | source)
XLA Modules:
  0.0 378.5 jit_solution(10559375372377683923)
XLA Ops:
  7.2 1.0 reshape.113.send_idx
  8.2 1.1 copy-done.2
  9.3 18.7 %send_gather.1 = (bf16[768,512]{1,0:T(8,128)(2,1)S(1)}, bf16[12288,128]{1,0:T(8,128)(2,1)}) custom-call(s32[12288]{0:T(1024)S(1)} %reshape.113.send_idx, bf16[3072,128]{1,0:T(8,128)(2,1)S(1)} %copy-done.2), custom_call_target="tpu_custom_call" | custom-call | tf_op jit(solution)/shard_map/send_gather/pallas_call | solution.py:230
  28.0 0.9 copy-done.13
  28.9 12.6 %all-to-all-start.1 = ((bf16[64,192,128]{2,1,0:T(8,128)(2,1)}), bf16[64,192,128]{2,1,0:T(8,128)(2,1)S(1)}, u32[]{:S(2)}, u32[]{:S(2)}) async-start(bf16[64,192,128]{2,1,0:T(8,128)(2,1)} %bitcast.11), calls=%async_computation.1 | async-start | bytes 6291456 | tf_op jit(solution)/shard_map/all_to_all | solution.py:283
  41.5 0.0 all-gather.3.cloned.1.call-start
  41.5 1.6 pad_maximum_fusion.1
  43.2 0.6 fusion.8
  43.9 1.5 fusion.6
  45.3 1.0 copy.22
  46.4 1.4 reshape.111
  47.9 1.5 fusion.5
  49.4 0.9 pad_maximum_fusion
  50.3 64.7 %all-to-all-done.1 = bf16[64,192,128]{2,1,0:T(8,128)(2,1)S(1)} async-done(((bf16[64,192,128]{2,1,0:T(8,128)(2,1)}), bf16[64,192,128]{2,1,0:T(8,128)(2,1)S(1)}, u32[]{:S(2)}, u32[]{:S(2)}) %all-to-all-start.1) | async-done | bytes 3145760 | tf_op jit(solution)/shard_map/all_to_all | solution.py:283
  115.0 6.2 %all-to-all-start = ((bf16[64,36,128]{2,1,0:T(8,128)(2,1)}), bf16[64,36,128]{2,1,0:T(8,128)(2,1)}, u32[]{:S(2)}, u32[]{:S(2)}) async-start(bf16[64,36,128]{2,1,0:T(8,128)(2,1)} %pad_maximum_fusion), calls=%async_computation | async-start | bytes 1310720 | tf_op jit(solution)/shard_map/all_to_all | solution.py:303
  121.2 1.0 reshape.107.neigh_idx
  122.2 0.0 all-gather.3.cloned.1.call-done.weights
  122.2 1.1 copy-done.3
  123.4 1.2 copy-done.6
  124.6 1.1 copy-done.14
  125.7 55.1 %layer_one.1 = (bf16[768,512]{1,0:T(8,128)(2,1)S(1)}, bf16[3072,128]{1,0:T(8,128)(2,1)S(1)}, bf16[12288,128]{1,0:T(8,128)(2,1)S(1)}) custom-call(s32[30720]{0:T(1024)S(1)} %reshape.107.neigh_idx, s32[12288]{0:T(1024)S(1)} %reshape.113.send_idx, bf16[3072,128]{1,0:T(8,128)(2,1)S(1)} %copy-done.3, bf16[12288,128]{1,0:T(8,128)(2,1)} %bitcast.45, ...), custom_call_target="tpu_custom_call" | custom-call | tf_op jit(solution)/shard_map/layer_one/pallas_call | solution.py:230
  180.9 1.6 copy-done.1
  182.5 0.9 copy-done.7
  183.4 0.9 copy-done.9
  184.3 11.8 %all-to-all-start.2 = ((bf16[64,192,128]{2,1,0:T(8,128)(2,1)}), bf16[64,192,128]{2,1,0:T(8,128)(2,1)S(1)}, u32[]{:S(2)}, u32[]{:S(2)}) async-start(bf16[64,192,128]{2,1,0:T(8,128)(2,1)} %bitcast.41), calls=%async_computation.2 | async-start | bytes 6291456 | tf_op jit(solution)/shard_map/all_to_all | solution.py:283
  196.0 0.2 all-gather.5.cloned.1.call-start
  196.3 1.6 pad_maximum_fusion.2
  198.0 1.5 slice.18
  199.5 1.0 copy.29
  200.6 0.8 copy.24
  201.4 1.1 reshape.112.items
  202.5 1.9 slice.21
  204.3 21.2 %all-gather.5.cloned.1.call-done.weights = bf16[1024,512]{1,0:T(8,128)(2,1)} async-done(((bf16[1024,128]{1,0:T(8,128)(2,1)}), bf16[1024,512]{1,0:T(8,128)(2,1)}) %all-gather.5.cloned.1.call-update) | async-done | bytes 1048592 | tf_op jit(solution)/shard_map/all_gather | solution.py:262
  225.5 44.0 %all-to-all-done.2 = bf16[64,192,128]{2,1,0:T(8,128)(2,1)S(1)} async-done(((bf16[64,192,128]{2,1,0:T(8,128)(2,1)}), bf16[64,192,128]{2,1,0:T(8,128)(2,1)S(1)}, u32[]{:S(2)}, u32[]{:S(2)}) %all-to-all-start.2) | async-done | bytes 3145760 | tf_op jit(solution)/shard_map/all_to_all | solution.py:283
  269.5 1.0 copy-done.4
  270.6 1.2 copy-done.5
  271.8 1.1 copy-done.8
  272.9 1.1 copy-done.10
  274.1 73.5 %layer_two.1 = (bf16[3072,128]{1,0:T(8,128)(2,1)S(1)}, f32[64,256]{1,0:T(8,128)S(1)}) custom-call(s32[30720]{0:T(1024)S(1)} %reshape.107.neigh_idx, s32[16384]{0:T(1024)S(1)} %reshape.112.items, bf16[3072,128]{1,0:T(8,128)(2,1)S(1)} %copy-done.10, bf16[12288,128]{1,0:T(8,128)(2,1)S(1)} %bitcast.40, bf16[768,512]{1,0:T(8,128)(2,1)S(1)} %copy-done.8, ...), custom_call_target="tpu_custom_call" | custom-call | tf_op jit(solution)/shard_map/layer_two/pallas_call | solution.py:230
  347.6 0.9 copy-done.11
  348.4 0.7 copy.25
  349.1 7.3 %all-to-all-start.3 = ((f32[64,1,256]{2,1,0:T(1,128)}), f32[64,1,256]{2,1,0:T(1,128)S(1)}, u32[]{:S(2)}, u32[]{:S(2)}) async-start(f32[64,1,256]{2,1,0:T(1,128)} %copy.25), calls=%async_computation.3 | async-start | bytes 131072 | tf_op jit(solution)/shard_map/all_to_all | solution.py:345
  356.4 9.8 %all-to-all-done.3 = f32[64,1,256]{2,1,0:T(1,128)S(1)} async-done(((f32[64,1,256]{2,1,0:T(1,128)}), f32[64,1,256]{2,1,0:T(1,128)S(1)}, u32[]{:S(2)}, u32[]{:S(2)}) %all-to-all-start.3) | async-done | bytes 65568 | tf_op jit(solution)/shard_map/all_to_all | solution.py:345
  366.2 0.1 copy.26
  366.3 0.9 copy.27
  367.2 2.8 gather_fusion
  370.0 0.8 copy.28
  370.8 0.9 copy.33
  (41 shorter events, 0.3 us)
Async XLA Ops:
  7.2 40.6 %copy-start = (bf16[256,128]{1,0:T(8,128)(2,1)S(1)}, bf16[256,128]{1,0:T(8,128)(2,1)}, u32[]{:S(2)}) copy-start(bf16[256,128]{1,0:T(8,128)(2,1)} %param.17) | copy-start | bytes 196612
  8.1 1.1 copy-start.2
  28.0 0.9 copy-start.13
  28.9 12.6 %copy-start.16 = (bf16[512,128]{1,0:T(8,128)(2,1)S(1)}, bf16[512,128]{1,0:T(8,128)(2,1)}, u32[]{:S(2)}) copy-start(bf16[512,128]{1,0:T(8,128)(2,1)} %param.14) | copy-start | bytes 393220
  28.9 14.3 %copy-start.19 = (s32[256,4]{0,1:T(4,128)S(1)}, s32[256,4]{0,1:T(4,128)}, u32[]{:S(2)}) copy-start(s32[256,4]{0,1:T(4,128)} %param.18) | copy-start | bytes 12292
  28.9 14.9 %copy-start.18 = (s32[256,4,8]{0,2,1:T(8,128)S(1)}, s32[256,4,8]{0,2,1:T(8,128)}, u32[]{:S(2)}) copy-start(s32[256,4,8]{0,2,1:T(8,128)} %param.19) | copy-start | bytes 98308
  28.9 86.1 %all-to-all-start.1 = ((bf16[64,192,128]{2,1,0:T(8,128)(2,1)}), bf16[64,192,128]{2,1,0:T(8,128)(2,1)S(1)}, u32[]{:S(2)}, u32[]{:S(2)}) async-start(bf16[64,192,128]{2,1,0:T(8,128)(2,1)} %bitcast.11), calls=%async_computation.1 | async-start | bytes 6291456 | tf_op jit(solution)/shard_map/all_to_all | solution.py:283
  41.5 80.7 %all-gather.3.cloned.1.call-start = ((), (), s32[]{:S(2)}) async-start(), calls=%async_computation.4 | async-start | bytes 1310720 | tf_op jit(solution)/shard_map/all_gather | solution.py:261
  115.0 7.2 %copy-start.15 = (bf16[64,192,128]{2,1,0:T(8,128)(2,1)}, bf16[64,192,128]{2,1,0:T(8,128)(2,1)S(1)}, u32[]{:S(2)}) copy-start(bf16[64,192,128]{2,1,0:T(8,128)(2,1)S(1)} %all-to-all-done.1) | copy-start | bytes 9437188
  115.0 69.3 %all-to-all-start = ((bf16[64,36,128]{2,1,0:T(8,128)(2,1)}), bf16[64,36,128]{2,1,0:T(8,128)(2,1)}, u32[]{:S(2)}, u32[]{:S(2)}) async-start(bf16[64,36,128]{2,1,0:T(8,128)(2,1)} %pad_maximum_fusion), calls=%async_computation | async-start | bytes 1310720 | tf_op jit(solution)/shard_map/all_to_all | solution.py:303
  122.2 1.1 copy-start.3
  123.4 1.2 copy-start.6
  124.6 1.1 copy-start.14
  180.9 1.6 copy-start.1
  182.5 0.9 copy-start.7
  183.4 0.9 copy-start.9
  184.3 12.0 %copy-start.17 = (bf16[512,128]{1,0:T(8,128)(2,1)S(1)}, bf16[512,128]{1,0:T(8,128)(2,1)}, u32[]{:S(2)}) copy-start(bf16[512,128]{1,0:T(8,128)(2,1)} %param.16) | copy-start | bytes 393220
  184.3 85.3 %all-to-all-start.2 = ((bf16[64,192,128]{2,1,0:T(8,128)(2,1)}), bf16[64,192,128]{2,1,0:T(8,128)(2,1)S(1)}, u32[]{:S(2)}, u32[]{:S(2)}) async-start(bf16[64,192,128]{2,1,0:T(8,128)(2,1)} %bitcast.41), calls=%async_computation.2 | async-start | bytes 6291456 | tf_op jit(solution)/shard_map/all_to_all | solution.py:283
  196.0 29.5 %all-gather.5.cloned.1.call-start = ((), (), s32[]{:S(2)}) async-start(), calls=%async_computation.5 | async-start | bytes 1310720 | tf_op jit(solution)/shard_map/all_gather | solution.py:262
  269.5 1.0 copy-start.4
  270.6 1.2 copy-start.5
  271.8 1.1 copy-start.8
  272.9 1.1 copy-start.10
  347.5 0.9 copy-start.11
  349.1 17.1 %all-to-all-start.3 = ((f32[64,1,256]{2,1,0:T(1,128)}), f32[64,1,256]{2,1,0:T(1,128)S(1)}, u32[]{:S(2)}, u32[]{:S(2)}) async-start(f32[64,1,256]{2,1,0:T(1,128)} %copy.25), calls=%async_computation.3 | async-start | bytes 131072 | tf_op jit(solution)/shard_map/all_to_all | solution.py:345
  366.3 4.5 %copy-start.12 = (bf16[3072,128]{1,0:T(8,128)(2,1)S(1)}, bf16[3072,128]{1,0:T(8,128)(2,1)}, u32[]{:S(2)}) copy-start(bf16[3072,128]{1,0:T(8,128)(2,1)} %copy-done.11) | copy-start | bytes 2359300
Sparse Core Ops, SparseCore 0:
  44.1 26.7 all-gather.2
  198.7 26.7 all-gather.4

commit v2 on v0

v2 whole, which is shorter than its diff:
```python
import functools

import jax
import jax.numpy as jnp
from jax import lax
from jax.experimental import pallas as pl
from jax.experimental.pallas import tpu as pltpu
from jax.sharding import PartitionSpec as P

MESH = pl.DeviceIdType.MESH
VMEM = pltpu.VMEM
F32 = jnp.float32
BF16 = jnp.bfloat16
LANE = 128
EPS = 1e-06
TILES = 3


def columns_of(which):
    return pl.ds(pl.multiple_of(which * LANE, LANE), LANE)


def rows_of(which, count):
    return pl.ds(pl.multiple_of(which * count, count), count)


class Ring:
    def __init__(self, ndom, nx, nz):
        self.ndom, self.nx, self.nz = ndom, nx, nz
        me = lax.axis_index("dom")
        self.me = me
        self.core = lax.rem(me, 2)
        self.z = lax.rem(lax.div(me, 2), nz)
        self.x = lax.div(me, 2 * nz)

    def offset(self, n):
        nz, nx = self.nz, self.nx
        i = lax.rem(n, nz)
        dz = nz // 2 + (1 - 2 * lax.rem(i, 2)) * lax.div(i + 1, 2)
        turn = lax.div(n, nz)
        return lax.rem(lax.div(turn, 2) + 1, nx), dz, 1 - lax.rem(turn, 2)

    def target(self, n):
        dx, dz, dc = self.offset(n)
        x = lax.rem(self.x + dx, self.nx)
        z = lax.rem(self.z + dz, self.nz)
        return (x * self.nz + z) * 2 + lax.rem(self.core + dc, 2)

    def source(self, n):
        dx, dz, dc = self.offset(n)
        x = lax.rem(self.x - dx + self.nx, self.nx)
        z = lax.rem(self.z - dz + self.nz, self.nz)
        return (x * self.nz + z) * 2 + lax.rem(self.core + dc, 2)


def to_dom(src, dst, send, recv, target):
    return pltpu.make_async_remote_copy(
        src_ref=src, dst_ref=dst, send_sem=send, recv_sem=recv,
        device_id={"dom": target}, device_id_type=MESH,
    )


def to_rep(src, dst, send, recv, target):
    return pltpu.make_async_remote_copy(
        src_ref=src, dst_ref=dst, send_sem=send, recv_sem=recv,
        device_id={"rep": target}, device_id_type=MESH,
    )


def pick_rows(index_of, table, stage, unroll):
    def some(block, carry):
        base = block * unroll
        for u in range(unroll):
            stage[pl.ds(base + u, 1), :] = table[pl.ds(index_of(base, u), 1), :]
        return carry

    lax.fori_loop(0, stage.shape[0] // unroll, some, 0)


def sum_rows(index_ref, start, table, stage, nodes, fan, unroll):
    def some(block, carry):
        base = block * unroll
        for u in range(unroll):
            terms = [
                table[pl.ds(index_ref[k * nodes + start + base + u], 1), :] for k in range(fan)
            ]
            while len(terms) > 1:
                pairs = [terms[i] + terms[i + 1] for i in range(0, len(terms) - 1, 2)]
                terms = pairs + terms[len(pairs) * 2 :]
            stage[pl.ds(base + u, 1), :] = terms[0]
        return carry

    lax.fori_loop(0, stage.shape[0] // unroll, some, 0)


def start_boundary(ring, send_idx, table, nodes, pick, outgoing, landing, send, recv):
    count = pick.shape[0]

    def one(n, carry):
        to = ring.target(n)
        pick_rows(lambda base, u: send_idx[to * count + base + u], table, pick, 32)
        outgoing[rows_of(to, count), :] = pick[...].astype(BF16)
        to_dom(
            outgoing.at[rows_of(to, count), :],
            landing.at[rows_of(ring.me, count), :],
            send.at[n],
            recv.at[n],
            to,
        ).start()
        return carry

    lax.fori_loop(0, ring.ndom - 1, one, 0)
    me = ring.me
    pick_rows(lambda base, u: send_idx[me * count + base + u], table, pick, 32)
    table[pl.ds(pl.multiple_of(nodes + me * count, 64), count), :] = pick[...]


def finish_boundary(ring, table, nodes, count, outgoing, landing, send, recv):
    def one(n, carry):
        to, source = ring.target(n), ring.source(n)
        copy = to_dom(
            outgoing.at[rows_of(to, count), :],
            landing.at[rows_of(source, count), :],
            send.at[n],
            recv.at[n],
            to,
        )
        copy.wait_recv()
        table[pl.ds(pl.multiple_of(nodes + source * count, 64), count), :] = landing[
            rows_of(source, count), :
        ].astype(F32)
        copy.wait_send()
        return carry

    lax.fori_loop(0, ring.ndom - 1, one, 0)


def layer(
    active, me, nrep, fan, neigh_idx, nodes, table, stage, before_product,
    self_rows, weights, chunks, agg_rows, hid_rows, hid_cols, send, recv, hsend, hrecv, local,
):
    chunk = nodes // nrep
    width = self_rows.shape[1]
    copies = []
    for step in range(nrep):
        to = lax.rem(me + 1 + step, nrep)
        sum_rows(neigh_idx, to * chunk, table, stage, nodes, fan, 16)
        chunks[step] = (stage[...] / fan).astype(BF16)
        there = agg_rows.at[:, columns_of(me)]
        if step < nrep - 1:
            copy = to_rep(chunks.at[step], there, send.at[step], recv.at[step], to)
        else:
            copy = pltpu.make_async_copy(chunks.at[step], there, local.at[0])
        copy.start()
        copies.append(copy)
    for copy in before_product + copies:
        copy.wait()
    tile = chunk // TILES
    back = []
    for t in range(TILES):
        rows = pl.ds(t * tile, tile)
        z = jnp.dot(self_rows[rows, :], weights[pl.ds(0, width), :], preferred_element_type=F32)
        z = z + jnp.dot(
            agg_rows[rows, :], weights[pl.ds(width, width), :], preferred_element_type=F32
        )
        if active:
            z = jnp.maximum(z, 0.0)
        mean = jnp.sum(z * z, axis=1, keepdims=True) / width
        hid_rows[rows, :] = (z * lax.rsqrt(mean + EPS)).astype(BF16)
        there = hid_cols.at[pl.ds(pl.multiple_of(me * chunk + t * tile, tile), tile), :]
        for step in range(nrep - 1):
            to = lax.rem(me + 1 + step, nrep)
            copy = to_rep(
                hid_rows.at[rows, columns_of(to)], there, hsend.at[t, step], hrecv.at[t, step], to
            )
            copy.start()
            back.append(copy)
        copy = pltpu.make_async_copy(hid_rows.at[rows, columns_of(me)], there, local.at[1 + t])
        copy.start()
        back.append(copy)
    for copy in back:
        copy.wait()
    table[pl.ds(0, nodes), :] = hid_cols[...].astype(F32)


def kernel(
    nrep, ndom, nx, nz, fan, nitems,
    neigh_idx, send_idx, own, wself1, wneigh1, wself2, wneigh2, asked, lists,
    embed, fetched,
    table, stage, pick, found, outgoing, landing1, landing2, chunks1, chunks2, agg1, agg2,
    x_rows, h_rows, e_rows, h_cols, weights1, weights2, got, got_lists, items, partial, total,
    bsend1, brecv1, bsend2, brecv2, qsend, qrecv, isend, irecv, fsend, frecv, xsend, xrecv, wsend, wrecv,
    psend, precv, asend1, arecv1, hsend1, hrecv1, local1, asend2, arecv2, hsend2, hrecv2, local2,
    local,
):
    ring = Ring(ndom, nx, nz)
    me = lax.axis_index("rep")
    nodes = own.shape[0]
    chunk = nodes // nrep
    full = h_rows.shape[1]

    barrier = pltpu.get_barrier_semaphore()

    def greet(n, carry):
        pl.semaphore_signal(barrier, inc=1, device_id={"dom": ring.target(n)}, device_id_type=MESH)
        return carry

    lax.fori_loop(0, ndom - 1, greet, 0)
    for step in range(1, nrep):
        pl.semaphore_signal(
            barrier, inc=1, device_id={"rep": lax.rem(me + step, nrep)}, device_id_type=MESH
        )
    table[pl.ds(0, nodes), :] = own[...].astype(F32)
    pl.semaphore_wait(barrier, ndom - 1 + nrep - 1)

    early = []
    blocks = (
        (wself1, weights1, 0), (wneigh1, weights1, full),
        (wself2, weights2, 0), (wneigh2, weights2, full),
    )
    for step in range(nrep - 1):
        to = lax.rem(me + 1 + step, nrep)
        early.append(
            to_rep(own.at[rows_of(to, chunk), :], x_rows.at[:, columns_of(me)],
                   xsend.at[step], xrecv.at[step], to)
        )
        for b, (part, whole, at) in enumerate(blocks):
            early.append(
                to_rep(part, whole.at[pl.ds(at, full), columns_of(me)],
                       wsend.at[b, step], wrecv.at[b, step], to)
            )
    early.append(
        pltpu.make_async_copy(own.at[rows_of(me, chunk), :], x_rows.at[:, columns_of(me)], local.at[0])
    )
    for b, (part, whole, at) in enumerate(blocks):
        early.append(
            pltpu.make_async_copy(part, whole.at[pl.ds(at, full), columns_of(me)], local.at[1 + b])
        )
    for copy in early:
        copy.start()

    count = pick.shape[0]
    start_boundary(ring, send_idx, table, nodes, pick, outgoing, landing1, bsend1, brecv1)
    finish_boundary(ring, table, nodes, count, outgoing, landing1, bsend1, brecv1)

    qrows = got.shape[0] // ndom
    own_asked = [
        pltpu.make_async_copy(
            asked.at[rows_of(ring.me, qrows), :], got.at[rows_of(ring.me, qrows), :],
            local.at[1 + len(blocks)],
        ),
        pltpu.make_async_copy(
            lists.at[ring.me], got_lists.at[ring.me], local.at[2 + len(blocks)]
        ),
    ]
    for copy in own_asked:
        copy.start()

    def query_copies(n, origin):
        to = ring.target(n)
        return (
            to_dom(asked.at[rows_of(to, qrows), :], got.at[rows_of(origin, qrows), :],
                   qsend.at[n], qrecv.at[n], to),
            to_dom(lists.at[to], got_lists.at[origin], isend.at[n], irecv.at[n], to),
        )

    def ask(n, carry):
        for copy in query_copies(n, ring.me):
            copy.start()
        return carry

    lax.fori_loop(0, ndom - 1, ask, 0)
    layer(
        True, me, nrep, fan, neigh_idx, nodes, table, stage, early, x_rows, weights1,
        chunks1, agg1, h_rows, h_cols, asend1, arecv1, hsend1, hrecv1, local1,
    )
    start_boundary(ring, send_idx, table, nodes, pick, outgoing, landing2, bsend2, brecv2)

    def asked_by(n, carry):
        for copy in query_copies(n, ring.source(n)):
            copy.wait()
        return carry

    lax.fori_loop(0, ndom - 1, asked_by, 0)
    for copy in own_asked:
        copy.wait()
    into = pltpu.make_async_copy(got_lists, items, local.at[3 + len(blocks)])
    into.start()
    into.wait()
    finish_boundary(ring, table, nodes, count, outgoing, landing2, bsend2, brecv2)
    layer(
        False, me, nrep, fan, neigh_idx, nodes, table, stage, [], h_rows, weights2,
        chunks2, agg2, e_rows, embed, asend2, arecv2, hsend2, hrecv2, local2,
    )

    slots = qrows
    half = got_lists.shape[1]
    wide = found.shape[0]
    owns = lax.broadcasted_iota(jnp.int32, (slots, wide), 0)
    slot = lax.rem(lax.broadcasted_iota(jnp.int32, (slots, wide), 1), slots)

    def score(p, carry):
        for h in range(half):
            pick_rows(
                lambda base, u: items[p, h, base + u],
                table, found.at[pl.ds(h * LANE, LANE), :], 32,
            )
        products = lax.dot_general(
            got[pl.ds(pl.multiple_of(p * qrows, 16), slots), :],
            found[...].astype(BF16),
            (((1,), (1,)), ((), ())),
            preferred_element_type=F32,
        )
        kept = jnp.sum(jnp.where(owns == slot, products, 0.0), axis=0, keepdims=True)
        for h in range(half):
            partial[me, p, pl.ds(h, 1), :] = kept[:, h * LANE : (h + 1) * LANE]
        return carry

    lax.fori_loop(0, ndom, score, 0)
    copies = []
    for step in range(nrep - 1):
        copy = to_rep(partial.at[me], partial.at[me], psend.at[step], precv.at[step],
                      lax.rem(me + 1 + step, nrep))
        copy.start()
        copies.append(copy)
    for copy in copies:
        copy.wait()
    added = partial[0]
    for other in range(1, nrep):
        added = added + partial[other]
    total[...] = added
    fetched[ring.me] = total[ring.me]

    def answer(n, carry):
        to = ring.target(n)
        to_dom(total.at[to], fetched.at[ring.me], fsend.at[n], frecv.at[n], to).start()
        return carry

    def answered(n, carry):
        to, source = ring.target(n), ring.source(n)
        to_dom(total.at[to], fetched.at[source], fsend.at[n], frecv.at[n], to).wait()
        return carry

    lax.fori_loop(0, ndom - 1, answer, 0)
    lax.fori_loop(0, ndom - 1, answered, 0)


def body(
    features, send_rows, neighbours, w_self1, w_neigh1, w_self2, w_neigh2, queries, owners, slate
):
    ndom, nrep = lax.axis_size("dom"), lax.axis_size("rep")
    nx, nz = 4, 8
    nodes, width = features.shape
    fan = neighbours.shape[1]
    per_pair = send_rows.shape[1]
    chunk = nodes // nrep
    full = width * nrep
    sessions, topq, nitems = slate.shape
    capacity = min(sessions, 2 * sessions * topq // ndom)
    entries, nslots = sessions * topq, ndom * capacity
    count = capacity * nitems
    half = count // LANE
    qrows = capacity

    send_idx = send_rows.reshape(-1)
    neigh_idx = neighbours.T.reshape(-1)

    owner_of = owners.T.reshape(entries)
    named = owner_of[:, None] == jnp.arange(ndom, dtype=jnp.int32)[None, :]
    order = jnp.arange(entries, dtype=jnp.int32)
    earlier = (order[:, None] > order[None, :]).astype(BF16)
    before = jnp.dot(earlier, named.astype(BF16), preferred_element_type=F32)
    position = jnp.sum(jnp.where(named, before, 0.0), axis=1).astype(jnp.int32)
    slot_index = owner_of * capacity + position
    place = (jnp.arange(nslots, dtype=jnp.int32)[:, None] == slot_index[None, :]).astype(BF16)
    slot_queries = jnp.dot(place, jnp.tile(queries, (topq, 1)), preferred_element_type=F32)
    asked = slot_queries.astype(BF16)
    lists = slate.transpose(1, 0, 2).reshape(entries, nitems)
    digits = jnp.concatenate([lists // 64, lists % 64], axis=1).astype(BF16)
    slot_digits = jnp.dot(place, digits, preferred_element_type=F32).astype(jnp.int32)
    slot_lists = slot_digits[:, :nitems] * 64 + slot_digits[:, nitems:]
    slot_lists = slot_lists.reshape(ndom, capacity, nitems).transpose(0, 2, 1)
    slot_lists = slot_lists.reshape(ndom, half, LANE)

    dma = pltpu.SemaphoreType.DMA
    shape = jax.ShapeDtypeStruct
    whole = pl.BlockSpec(memory_space=VMEM)
    peers, others = (ndom - 1,), (nrep - 1,)
    args = [neigh_idx, send_idx, features, w_self1, w_neigh1, w_self2, w_neigh2, asked, slot_lists]
    per_layer = [dma(others), dma(others), dma((TILES, nrep - 1)), dma((TILES, nrep - 1)), dma((1 + TILES,))]
    node_embed, fetched = pl.pallas_call(
        functools.partial(kernel, nrep, ndom, nx, nz, fan, nitems),
        out_shape=[shape((nodes, width), BF16), shape((ndom, half, LANE), F32)],
        in_specs=[pl.BlockSpec(memory_space=pltpu.SMEM)] * 2 + [whole] * (len(args) - 2),
        out_specs=[whole, whole],
        scratch_shapes=[
            VMEM((nodes + ndom * per_pair, width), F32),
            VMEM((chunk, width), F32),
            VMEM((per_pair, width), F32),
            VMEM((count, width), F32),
            VMEM((ndom * per_pair, width), BF16),
            VMEM((ndom * per_pair, width), BF16),
            VMEM((ndom * per_pair, width), BF16),
            VMEM((nrep, chunk, width), BF16),
            VMEM((nrep, chunk, width), BF16),
            VMEM((chunk, full), BF16),
            VMEM((chunk, full), BF16),
            VMEM((chunk, full), BF16),
            VMEM((chunk, full), BF16),
            VMEM((chunk, full), BF16),
            VMEM((nodes, width), BF16),
            VMEM((2 * full, full), BF16),
            VMEM((2 * full, full), BF16),
            VMEM((ndom * qrows, LANE), BF16),
            VMEM((ndom, half, LANE), jnp.int32),
            pltpu.SMEM((ndom, half, LANE), jnp.int32),
            VMEM((nrep, ndom, half, LANE), F32),
            VMEM((ndom, half, LANE), F32),
        ]
        + [dma(peers)] * 10
        + [dma(others)] * 2
        + [dma((4, nrep - 1))] * 2
        + [dma(others)] * 2
        + per_layer
        + per_layer
        + [dma((9,))],
        compiler_params=pltpu.CompilerParams(
            collective_id=1, has_side_effects=True, vmem_limit_bytes=56 * 1024 * 1024
        ),
        name="graph_and_scores",
    )(*args)
    fetched = fetched.reshape(ndom, nitems, capacity).transpose(0, 2, 1).reshape(nslots, nitems)
    scores = fetched[slot_index].reshape(topq, sessions, nitems)
    return (node_embed, scores.transpose(1, 0, 2).reshape(sessions, topq * nitems))


def solution(mesh):
    placed = (
        P("dom", "rep"),
        P("dom", None),
        P("dom", None),
        P(None, "rep"),
        P(None, "rep"),
        P(None, "rep"),
        P(None, "rep"),
        P("dom", "rep"),
        P("dom", None),
        P("dom", None, None),
    )
    return jax.shard_map(
        body,
        mesh=mesh,
        in_specs=placed,
        out_specs=(P("dom", "rep"), P("dom", None)),
        check_vma=False,
    )
```

time: 852 us -> 317 us (0.37)
  local copies, waits for them, and re-layouts: 408 us -> 9.49 us
  Pallas kernels: 0 us -> 302 us
  waiting for transfers between devices: 275 us -> 0 us
  blocking collectives: 53.2 us -> 0 us
  starting transfers between devices: 44.3 us -> 0 us
  other arithmetic: 40.7 us -> 0.08 us
  between operations: 14.3 us -> 0.81 us
  matrix products: 13.2 us -> 4.4 us
    gather x24 -> x1, local copies, waits for them, and re-layouts: 399 us -> 2.81 us  [body(): scores = fetched[slot_index].reshape(topq, sessions, nitems)]
    pallas_call x0 -> x1, Pallas kernels: none -> 302 us  [body(): pl.pallas_call(functools.partial(kernel, nrep, ndom, nx, nz, fan, nitems)...]
    all_to_all x3 -> x0, waiting for transfers between devices: 220 us -> none  [the longest x2 125 us: sage_layer(): lax.all_to_all(outgoing, 'dom', split_axis=0, concat_axis=0, tiled=True)]
    all_gather x4 -> x0, waiting for transfers between devices: 53 us -> none  [the longest x2 52.9 us: sage_layer(): lax.all_gather(agg, 'rep', axis=1, tiled=True)]
    all_to_all x3 -> x0, starting transfers between devices: 44.1 us -> none  [the longest x2 28.8 us: sage_layer(): lax.all_to_all(outgoing, 'dom', split_axis=0, concat_axis=0, tiled=True)]
    psum x3 -> x0, blocking collectives: 37.6 us -> none  [the longest x2 25 us: sage_layer(): squares = lax.psum(jnp.sum(z * z, axis=1), 'rep')]
    another operation x3 -> x1, other arithmetic: 18.2 us -> 0.04 us
    all_to_all x1 -> x0, blocking collectives: 15.7 us -> none  [body(): lax.all_to_all(send_lists, 'dom', split_axis=0, concat_axis=0, tiled=True)]
  transfers between devices with their start and end apart: 7 -> 0, of which waited for: 5 -> 0; matrix products, arithmetic and copies ran while one was open for 36% -> 0% of each run, Pallas kernels for 0% -> 0%
where the time goes in v2:
time: 317 us
  Pallas kernels  302 us (95%)
  local copies, waits for them, and re-layouts  9.49 us (3%)
  matrix products  4.4 us (1%)
    pallas_call x1, Pallas kernels, body(): pl.pallas_call(functools.partial(kernel, nrep, ndom, nx, nz, fan, nitems)...  302 us

profile of v2, /device:TPU:1, one launch (start us, length us, event | category | flops | bytes accessed | tf_op | source)
XLA Modules:
  0.0 317.0 jit_solution(17605394120594534702)
XLA Ops:
  0.6 0.0 copy-start
  0.6 0.0 copy-start.5
  0.7 0.0 copy-start.4
  0.7 0.0 copy-start.3
  0.7 0.7 copy.20
  1.4 0.6 fusion.8
  2.0 0.0 copy-done.5
  2.1 0.0 copy-done.4
  2.2 0.0 copy-done.3
  2.2 0.7 reshape.81.send_idx
  2.9 0.0 copy-start.2
  2.9 1.5 fusion.6
  4.4 0.0 copy-done.2
  4.4 0.7 reshape.80.neigh_idx
  5.1 0.1 reshape.84
  5.2 0.1 copy.15
  5.3 0.7 copy.16.lists
  6.0 0.0 copy-done
  6.0 2.3 fusion.5.asked
  8.4 302.2 %graph_and_scores.1 = (bf16[3072,128]{1,0:T(8,128)(2,1)}, f32[64,2,128]{2,1,0:T(2,128)}) custom-call(s32[30720]{0:T(1024)} %reshape.80.neigh_idx, s32[12288]{0:T(1024)} %reshape.81.send_idx, bf16[3072,128]{1,0:T(8,128)(2,1)} %own.1, bf16[512,128]{1,0:T(8,128)(2,1)} %wself1.1, bf16[512,128]{1,0:T(8,128)(2,1)} %wneigh1.1, bf16[512,128]{1,0:T(8,128)(2,1)} %wself2.1, ...), custom_call_target="tpu_custom_call" | custom-call | tf_op jit(solution)/shard_map/graph_and_scores/pallas_call | solution.py:391
  310.6 0.9 copy.17
  311.5 0.9 copy.18
  312.5 0.0 copy-start.1
  312.5 2.8 gather_fusion
  315.3 0.8 copy.19
  316.1 0.0 copy-done.1
  316.1 0.9 copy.23
  (9 shorter events, 0.1 us)
Async XLA Ops:
  0.6 5.4 %copy-start = (bf16[256,128]{1,0:T(8,128)(2,1)S(1)}, bf16[256,128]{1,0:T(8,128)(2,1)}, u32[]{:S(2)}) copy-start(bf16[256,128]{1,0:T(8,128)(2,1)} %param.17) | copy-start | bytes 196612
  0.6 1.4 copy-start.5
  0.7 1.5 copy-start.4
  0.7 1.5 copy-start.3
  2.9 1.5 copy-start.2
  312.5 3.6 %copy-start.1 = (bf16[3072,128]{1,0:T(8,128)(2,1)S(1)}, bf16[3072,128]{1,0:T(8,128)(2,1)}, u32[]{:S(2)}) copy-start(bf16[3072,128]{1,0:T(8,128)(2,1)} %get-tuple-element.10) | copy-start | bytes 2359300

commit v3 on v2

--- a/solution.py
+++ b/solution.py
@@ -13,7 +13,7 @@
 BF16 = jnp.bfloat16
 LANE = 128
 EPS = 1e-06
-TILES = 3
+TILES = 4
 
 
 def columns_of(which):
@@ -141,23 +141,39 @@
 ):
     chunk = nodes // nrep
     width = self_rows.shape[1]
-    copies = []
-    for step in range(nrep):
+    tile = chunk // TILES
+
+    def there(t):
+        return agg_rows.at[pl.ds(t * tile, tile), columns_of(me)]
+
+    def sum_copy(t, step):
         to = lax.rem(me + 1 + step, nrep)
-        sum_rows(neigh_idx, to * chunk, table, stage, nodes, fan, 16)
-        chunks[step] = (stage[...] / fan).astype(BF16)
-        there = agg_rows.at[:, columns_of(me)]
-        if step < nrep - 1:
-            copy = to_rep(chunks.at[step], there, send.at[step], recv.at[step], to)
-        else:
-            copy = pltpu.make_async_copy(chunks.at[step], there, local.at[0])
-        copy.start()
-        copies.append(copy)
-    for copy in before_product + copies:
-        copy.wait()
-    tile = chunk // TILES
+        return to_rep(chunks.at[t, step], there(t), send.at[t, step], recv.at[t, step], to)
+
+    def own_sum_copy(t):
+        return pltpu.make_async_copy(chunks.at[t, nrep - 1], there(t), local.at[0, t])
+
+    def sums(t):
+        def summed(step):
+            to = lax.rem(me + 1 + step, nrep)
+            sum_rows(neigh_idx, to * chunk + t * tile, table, stage, nodes, fan, 16)
+            chunks[t, step] = (stage[...] / fan).astype(BF16)
+
+        def one(step, carry):
+            summed(step)
+            sum_copy(t, step).start()
+            return carry
+
+        lax.fori_loop(0, nrep - 1, one, 0)
+        summed(nrep - 1)
+        own_sum_copy(t).start()
+
     back = []
-    for t in range(TILES):
+
+    def product(t):
+        for step in range(nrep - 1):
+            sum_copy(t, step).wait()
+        own_sum_copy(t).wait()
         rows = pl.ds(t * tile, tile)
         z = jnp.dot(self_rows[rows, :], weights[pl.ds(0, width), :], preferred_element_type=F32)
         z = z + jnp.dot(
@@ -167,17 +183,25 @@
             z = jnp.maximum(z, 0.0)
         mean = jnp.sum(z * z, axis=1, keepdims=True) / width
         hid_rows[rows, :] = (z * lax.rsqrt(mean + EPS)).astype(BF16)
-        there = hid_cols.at[pl.ds(pl.multiple_of(me * chunk + t * tile, tile), tile), :]
+        landing = hid_cols.at[pl.ds(pl.multiple_of(me * chunk + t * tile, tile), tile), :]
         for step in range(nrep - 1):
             to = lax.rem(me + 1 + step, nrep)
             copy = to_rep(
-                hid_rows.at[rows, columns_of(to)], there, hsend.at[t, step], hrecv.at[t, step], to
+                hid_rows.at[rows, columns_of(to)], landing, hsend.at[t, step], hrecv.at[t, step], to
             )
             copy.start()
             back.append(copy)
-        copy = pltpu.make_async_copy(hid_rows.at[rows, columns_of(me)], there, local.at[1 + t])
+        copy = pltpu.make_async_copy(hid_rows.at[rows, columns_of(me)], landing, local.at[1, t])
         copy.start()
         back.append(copy)
+
+    sums(0)
+    for copy in before_product:
+        copy.wait()
+    for t in range(1, TILES):
+        sums(t)
+        product(t - 1)
+    product(TILES - 1)
     for copy in back:
         copy.wait()
     table[pl.ds(0, nodes), :] = hid_cols[...].astype(F32)
@@ -295,28 +319,35 @@
 
     slots = qrows
     half = got_lists.shape[1]
-    wide = found.shape[0]
+    wide = half * LANE
     owns = lax.broadcasted_iota(jnp.int32, (slots, wide), 0)
     slot = lax.rem(lax.broadcasted_iota(jnp.int32, (slots, wide), 1), slots)
 
-    def score(p, carry):
+    def find(p, carry):
+        base = pl.multiple_of(p * wide, wide)
         for h in range(half):
-            pick_rows(
-                lambda base, u: items[p, h, base + u],
-                table, found.at[pl.ds(h * LANE, LANE), :], 32,
+            for i in range(LANE):
+                found[pl.ds(base + (h * LANE + i), 1), :] = table[pl.ds(items[p, h, i], 1), :]
+        return carry
+
+    lax.fori_loop(0, ndom, find, 0)
+    together = 4
+
+    def score(block, carry):
+        for u in range(together):
+            p = block * together + u
+            products = lax.dot_general(
+                got[rows_of(p, slots), :],
+                found[rows_of(p, wide), :].astype(BF16),
+                (((1,), (1,)), ((), ())),
+                preferred_element_type=F32,
             )
-        products = lax.dot_general(
-            got[pl.ds(pl.multiple_of(p * qrows, 16), slots), :],
-            found[...].astype(BF16),
-            (((1,), (1,)), ((), ())),
-            preferred_element_type=F32,
-        )
-        kept = jnp.sum(jnp.where(owns == slot, products, 0.0), axis=0, keepdims=True)
-        for h in range(half):
-            partial[me, p, pl.ds(h, 1), :] = kept[:, h * LANE : (h + 1) * LANE]
-        return carry
-
-    lax.fori_loop(0, ndom, score, 0)
+            kept = jnp.sum(jnp.where(owns == slot, products, 0.0), axis=0, keepdims=True)
+            for h in range(half):
+                partial[me, p, pl.ds(h, 1), :] = kept[:, h * LANE : (h + 1) * LANE]
+        return carry
+
+    lax.fori_loop(0, ndom // together, score, 0)
     copies = []
     for step in range(nrep - 1):
         copy = to_rep(partial.at[me], partial.at[me], psend.at[step], precv.at[step],
@@ -387,7 +418,7 @@
     whole = pl.BlockSpec(memory_space=VMEM)
     peers, others = (ndom - 1,), (nrep - 1,)
     args = [neigh_idx, send_idx, features, w_self1, w_neigh1, w_self2, w_neigh2, asked, slot_lists]
-    per_layer = [dma(others), dma(others), dma((TILES, nrep - 1)), dma((TILES, nrep - 1)), dma((1 + TILES,))]
+    per_layer = [dma((TILES, nrep - 1))] * 4 + [dma((2, TILES))]
     node_embed, fetched = pl.pallas_call(
         functools.partial(kernel, nrep, ndom, nx, nz, fan, nitems),
         out_shape=[shape((nodes, width), BF16), shape((ndom, half, LANE), F32)],
@@ -395,14 +426,14 @@
         out_specs=[whole, whole],
         scratch_shapes=[
             VMEM((nodes + ndom * per_pair, width), F32),
-            VMEM((chunk, width), F32),
+            VMEM((chunk // TILES, width), F32),
             VMEM((per_pair, width), F32),
-            VMEM((count, width), F32),
+            VMEM((ndom * count, width), F32),
             VMEM((ndom * per_pair, width), BF16),
             VMEM((ndom * per_pair, width), BF16),
             VMEM((ndom * per_pair, width), BF16),
-            VMEM((nrep, chunk, width), BF16),
-            VMEM((nrep, chunk, width), BF16),
+            VMEM((TILES, nrep, chunk // TILES, width), BF16),
+            VMEM((TILES, nrep, chunk // TILES, width), BF16),
             VMEM((chunk, full), BF16),
             VMEM((chunk, full), BF16),
             VMEM((chunk, full), BF16),

time: 317 us -> 280 us (0.88)
  Pallas kernels: 302 us -> 265 us
    pallas_call x1, Pallas kernels: 302 us -> 265 us  [body(): pl.pallas_call(functools.partial(kernel, nrep, ndom, nx, nz, fan, nitems)...]
where the time goes in v3:
time: 280 us
  Pallas kernels  265 us (95%)
  local copies, waits for them, and re-layouts  9.49 us (3%)
  matrix products  4.4 us (2%)
    pallas_call x1, Pallas kernels, body(): pl.pallas_call(functools.partial(kernel, nrep, ndom, nx, nz, fan, nitems)...  265 us

profile of v3, /device:TPU:1, one launch (start us, length us, event | category | flops | bytes accessed | tf_op | source)
XLA Modules:
  0.0 279.9 jit_solution(10748690024020057183)
XLA Ops:
  0.6 0.0 copy-start
  0.6 0.0 copy-start.5
  0.7 0.0 copy-start.4
  0.7 0.0 copy-start.3
  0.7 0.7 copy.20
  1.4 0.6 fusion.8
  2.0 0.0 copy-done.5
  2.1 0.0 copy-done.4
  2.2 0.0 copy-done.3
  2.2 0.7 reshape.81.send_idx
  2.9 0.0 copy-start.2
  2.9 1.5 fusion.6
  4.4 0.0 copy-done.2
  4.4 0.7 reshape.80.neigh_idx
  5.1 0.1 reshape.84
  5.2 0.1 copy.15
  5.3 0.7 copy.16.lists
  6.0 0.0 copy-done
  6.0 2.3 fusion.5.asked
  8.4 265.1 %graph_and_scores.1 = (bf16[3072,128]{1,0:T(8,128)(2,1)}, f32[64,2,128]{2,1,0:T(2,128)}) custom-call(s32[30720]{0:T(1024)} %reshape.80.neigh_idx, s32[12288]{0:T(1024)} %reshape.81.send_idx, bf16[3072,128]{1,0:T(8,128)(2,1)} %own.1, bf16[512,128]{1,0:T(8,128)(2,1)} %wself1.1, bf16[512,128]{1,0:T(8,128)(2,1)} %wneigh1.1, bf16[512,128]{1,0:T(8,128)(2,1)} %wself2.1, ...), custom_call_target="tpu_custom_call" | custom-call | tf_op jit(solution)/shard_map/graph_and_scores/pallas_call | solution.py:422
  273.5 0.9 copy.17
  274.4 0.9 copy.18
  275.4 0.0 copy-start.1
  275.4 2.8 %gather_fusion = f32[1024,8]{1,0:T(8,128)S(1)} fusion(f32[2048,8]{1,0:T(8,128)S(1)} %bitcast.31, s32[1024]{0:T(1024)S(1)} %broadcast_clamp_fusion), kind=kCustom, calls=%fused_computation | custom fusion | bytes 69632 | tf_op jit(solution)/shard_map/gather | solution.py:464
  278.2 0.8 copy.19
  279.0 0.0 copy-done.1
  279.0 0.9 copy.23
  (9 shorter events, 0.1 us)
Async XLA Ops:
  0.6 5.4 %copy-start = (bf16[256,128]{1,0:T(8,128)(2,1)S(1)}, bf16[256,128]{1,0:T(8,128)(2,1)}, u32[]{:S(2)}) copy-start(bf16[256,128]{1,0:T(8,128)(2,1)} %param.17) | copy-start | bytes 196612
  0.6 1.4 copy-start.5
  0.7 1.5 copy-start.4
  0.7 1.5 copy-start.3
  2.9 1.5 copy-start.2
  275.4 3.6 %copy-start.1 = (bf16[3072,128]{1,0:T(8,128)(2,1)S(1)}, bf16[3072,128]{1,0:T(8,128)(2,1)}, u32[]{:S(2)}) copy-start(bf16[3072,128]{1,0:T(8,128)(2,1)} %get-tuple-element.10) | copy-start | bytes 2359300

commit v4 on v3

--- a/solution.py
+++ b/solution.py
@@ -78,11 +78,14 @@
 
 
 def sum_rows(index_ref, start, table, stage, nodes, fan, unroll):
+    span = nodes - unroll + 1
+
     def some(block, carry):
         base = block * unroll
         for u in range(unroll):
             terms = [
-                table[pl.ds(index_ref[k * nodes + start + base + u], 1), :] for k in range(fan)
+                table[pl.ds(index_ref.at[pl.ds(k * nodes + u, span)][start + base], 1), :]
+                for k in range(fan)
             ]
             while len(terms) > 1:
                 pairs = [terms[i] + terms[i + 1] for i in range(0, len(terms) - 1, 2)]
@@ -156,7 +159,7 @@
     def sums(t):
         def summed(step):
             to = lax.rem(me + 1 + step, nrep)
-            sum_rows(neigh_idx, to * chunk + t * tile, table, stage, nodes, fan, 16)
+            sum_rows(neigh_idx, to * chunk + t * tile, table, stage, nodes, fan, 32)
             chunks[t, step] = (stage[...] / fan).astype(BF16)
 
         def one(step, carry):
@@ -209,10 +212,10 @@
 
 def kernel(
     nrep, ndom, nx, nz, fan, nitems,
-    neigh_idx, send_idx, own, wself1, wneigh1, wself2, wneigh2, asked, lists,
-    embed, fetched,
+    neigh_idx, send_idx, own, wself1, wneigh1, wself2, wneigh2, queries, lists, slot_of,
+    embed, scores,
     table, stage, pick, found, outgoing, landing1, landing2, chunks1, chunks2, agg1, agg2,
-    x_rows, h_rows, e_rows, h_cols, weights1, weights2, got, got_lists, items, partial, total,
+    x_rows, h_rows, e_rows, h_cols, weights1, weights2, got, got_lists, items, partial, total, fetched, asked,
     bsend1, brecv1, bsend2, brecv2, qsend, qrecv, isend, irecv, fsend, frecv, xsend, xrecv, wsend, wrecv,
     psend, precv, asend1, arecv1, hsend1, hrecv1, local1, asend2, arecv2, hsend2, hrecv2, local2,
     local,
@@ -265,6 +268,19 @@
 
     count = pick.shape[0]
     start_boundary(ring, send_idx, table, nodes, pick, outgoing, landing1, bsend1, brecv1)
+    sessions = queries.shape[0]
+    topq = slot_of.shape[0]
+
+    def fill(block, carry):
+        slot = lax.broadcasted_iota(jnp.int32, (sessions, sessions), 0) + block * sessions
+        rows = jnp.zeros((sessions, LANE), F32)
+        for t in range(topq):
+            place = jnp.where(slot_of[t : t + 1, :] == slot, 1.0, 0.0).astype(BF16)
+            rows = rows + jnp.dot(place, queries[...], preferred_element_type=F32)
+        asked[rows_of(block, sessions), :] = rows.astype(BF16)
+        return carry
+
+    lax.fori_loop(0, asked.shape[0] // sessions, fill, 0)
     finish_boundary(ring, table, nodes, count, outgoing, landing1, bsend1, brecv1)
 
     qrows = got.shape[0] // ndom
@@ -327,7 +343,8 @@
         base = pl.multiple_of(p * wide, wide)
         for h in range(half):
             for i in range(LANE):
-                found[pl.ds(base + (h * LANE + i), 1), :] = table[pl.ds(items[p, h, i], 1), :]
+                item = items.at[:, pl.ds(h, 1), pl.ds(i, 1)][p, 0, 0]
+                found[pl.ds(base + (h * LANE + i), 1), :] = table[pl.ds(item, 1), :]
         return carry
 
     lax.fori_loop(0, ndom, find, 0)
@@ -374,6 +391,31 @@
 
     lax.fori_loop(0, ndom - 1, answer, 0)
     lax.fori_loop(0, ndom - 1, answered, 0)
+
+    parts = []
+    for h in range(half):
+        rest, split = fetched[:, h, :], []
+        for _ in range(3):
+            split.append(rest.astype(BF16))
+            rest = rest - split[-1].astype(F32)
+        parts.append(split)
+    partition = lax.broadcasted_iota(jnp.int32, (ndom, sessions), 0)
+    position = lax.rem(lax.broadcasted_iota(jnp.int32, (LANE, sessions), 0), slots)
+    each = LANE // slots
+    for t in range(topq):
+        entry = slot_of[t : t + 1, :]
+        owner = jnp.where(lax.div(entry, slots) == partition, 1.0, 0.0).astype(BF16)
+        for h in range(half):
+            answer_rows = jnp.zeros((LANE, sessions), F32)
+            for piece in parts[h]:
+                answer_rows = answer_rows + lax.dot_general(
+                    piece, owner, (((0,), (0,)), ((), ())), preferred_element_type=F32
+                )
+            kept = jnp.where(lax.rem(entry, slots) == position, answer_rows, 0.0)
+            for i in range(each):
+                scores[pl.ds(t * nitems + h * each + i, 1), :] = jnp.sum(
+                    kept[i * slots : (i + 1) * slots, :], axis=0, keepdims=True
+                )
 
 
 def body(
@@ -404,8 +446,6 @@
     position = jnp.sum(jnp.where(named, before, 0.0), axis=1).astype(jnp.int32)
     slot_index = owner_of * capacity + position
     place = (jnp.arange(nslots, dtype=jnp.int32)[:, None] == slot_index[None, :]).astype(BF16)
-    slot_queries = jnp.dot(place, jnp.tile(queries, (topq, 1)), preferred_element_type=F32)
-    asked = slot_queries.astype(BF16)
     lists = slate.transpose(1, 0, 2).reshape(entries, nitems)
     digits = jnp.concatenate([lists // 64, lists % 64], axis=1).astype(BF16)
     slot_digits = jnp.dot(place, digits, preferred_element_type=F32).astype(jnp.int32)
@@ -417,11 +457,12 @@
     shape = jax.ShapeDtypeStruct
     whole = pl.BlockSpec(memory_space=VMEM)
     peers, others = (ndom - 1,), (nrep - 1,)
-    args = [neigh_idx, send_idx, features, w_self1, w_neigh1, w_self2, w_neigh2, asked, slot_lists]
+    args = [neigh_idx, send_idx, features, w_self1, w_neigh1, w_self2, w_neigh2, queries, slot_lists]
+    args.append(slot_index.reshape(topq, sessions))
     per_layer = [dma((TILES, nrep - 1))] * 4 + [dma((2, TILES))]
-    node_embed, fetched = pl.pallas_call(
+    node_embed, scores = pl.pallas_call(
         functools.partial(kernel, nrep, ndom, nx, nz, fan, nitems),
-        out_shape=[shape((nodes, width), BF16), shape((ndom, half, LANE), F32)],
+        out_shape=[shape((nodes, width), BF16), shape((topq * nitems, sessions), F32)],
         in_specs=[pl.BlockSpec(memory_space=pltpu.SMEM)] * 2 + [whole] * (len(args) - 2),
         out_specs=[whole, whole],
         scratch_shapes=[
@@ -447,6 +488,8 @@
             pltpu.SMEM((ndom, half, LANE), jnp.int32),
             VMEM((nrep, ndom, half, LANE), F32),
             VMEM((ndom, half, LANE), F32),
+            VMEM((ndom, half, LANE), F32),
+            VMEM((ndom * qrows, LANE), BF16),
         ]
         + [dma(peers)] * 10
         + [dma(others)] * 2
@@ -460,9 +503,7 @@
         ),
         name="graph_and_scores",
     )(*args)
-    fetched = fetched.reshape(ndom, nitems, capacity).transpose(0, 2, 1).reshape(nslots, nitems)
-    scores = fetched[slot_index].reshape(topq, sessions, nitems)
-    return (node_embed, scores.transpose(1, 0, 2).reshape(sessions, topq * nitems))
+    return (node_embed, scores.T)
 
 
 def solution(mesh):

time: 280 us -> 253 us (0.904)
  Pallas kernels: 265 us -> 243 us
  local copies, waits for them, and re-layouts: 9.49 us -> 5.77 us
    pallas_call x1, Pallas kernels: 265 us -> 243 us  [body(): pl.pallas_call(functools.partial(kernel, nrep, ndom, nx, nz, fan, nitems)...]
    gather x1 -> x0, local copies, waits for them, and re-layouts: 2.81 us -> none  [body(): scores = fetched[slot_index].reshape(topq, sessions, nitems)]
where the time goes in v4:
time: 253 us; the launch traced here: 252 us
  Pallas kernels  243 us (96%)
  local copies, waits for them, and re-layouts  5.77 us (2%)
    pallas_call x1, Pallas kernels, body(): pl.pallas_call(functools.partial(kernel, nrep, ndom, nx, nz, fan, nitems)...  243 us

profile of v4, /device:TPU:1, one launch (start us, length us, event | category | flops | bytes accessed | tf_op | source)
XLA Modules:
  0.0 252.5 jit_solution(2161532525017950785)
XLA Ops:
  0.6 0.7 copy.15
  1.3 0.0 copy-start.4
  1.3 0.0 copy-start.2
  1.3 0.0 copy-start.1
  1.3 0.6 fusion.5
  2.0 0.0 copy-done.4
  2.0 0.6 fusion.14.slot_of
  2.6 0.0 copy-done.2
  2.6 0.0 copy-done.1
  2.7 0.7 reshape.36.send_idx
  3.4 0.0 copy-start
  3.4 1.5 fusion.3
  4.9 0.0 copy-done
  4.9 0.7 reshape.35.neigh_idx
  5.5 0.1 reshape.39
  5.7 0.1 copy.13
  5.8 0.7 copy.14.lists
  6.5 243.3 %graph_and_scores.1 = (bf16[3072,128]{1,0:T(8,128)(2,1)}, f32[32,256]{1,0:T(8,128)}) custom-call(s32[30720]{0:T(1024)} %reshape.35.neigh_idx, s32[12288]{0:T(1024)} %reshape.36.send_idx, bf16[3072,128]{1,0:T(8,128)(2,1)} %own.1, bf16[512,128]{1,0:T(8,128)(2,1)} %wself1.1, bf16[512,128]{1,0:T(8,128)(2,1)} %wneigh1.1, bf16[512,128]{1,0:T(8,128)(2,1)} %wself2.1, ...), custom_call_target="tpu_custom_call" | custom-call | tf_op jit(solution)/shard_map/graph_and_scores/pallas_call | solution.py:463
  249.8 0.0 copy-start.3
  249.8 2.1 copy.18
  251.9 0.0 copy-done.3
  251.9 0.6 copy.19
  (5 shorter events, 0.1 us)
Async XLA Ops:
  1.3 0.7 copy-start.4
  1.3 1.3 copy-start.2
  1.3 1.3 copy-start.1
  3.4 1.5 copy-start
  249.8 2.1 copy-start.3

commit v5 on v4

--- a/solution.py
+++ b/solution.py
@@ -14,6 +14,7 @@
 LANE = 128
 EPS = 1e-06
 TILES = 4
+SHARES = 4
 
 
 def columns_of(which):
@@ -51,6 +52,19 @@
         x = lax.rem(self.x - dx + self.nx, self.nx)
         z = lax.rem(self.z - dz + self.nz, self.nz)
         return (x * self.nz + z) * 2 + lax.rem(self.core + dc, 2)
+
+
+def for_peers(ndom, me, act):
+    peers = ndom - 1
+    together = 7 if peers % 7 == 0 else 1
+
+    def some(block, carry):
+        for u in range(together):
+            n = block * together + u
+            act(n, lax.rem(me + 1 + n, ndom), lax.rem(me + ndom - 1 - n, ndom))
+        return carry
+
+    lax.fori_loop(0, peers // together, some, 0)
 
 
 def to_dom(src, dst, send, recv, target):
@@ -228,11 +242,10 @@
 
     barrier = pltpu.get_barrier_semaphore()
 
-    def greet(n, carry):
-        pl.semaphore_signal(barrier, inc=1, device_id={"dom": ring.target(n)}, device_id_type=MESH)
-        return carry
-
-    lax.fori_loop(0, ndom - 1, greet, 0)
+    def greet(n, to, source):
+        pl.semaphore_signal(barrier, inc=1, device_id={"dom": to}, device_id_type=MESH)
+
+    for_peers(ndom, ring.me, greet)
     for step in range(1, nrep):
         pl.semaphore_signal(
             barrier, inc=1, device_id={"rep": lax.rem(me + step, nrep)}, device_id_type=MESH
@@ -296,32 +309,29 @@
     for copy in own_asked:
         copy.start()
 
-    def query_copies(n, origin):
-        to = ring.target(n)
+    def query_copies(n, to, origin):
         return (
             to_dom(asked.at[rows_of(to, qrows), :], got.at[rows_of(origin, qrows), :],
                    qsend.at[n], qrecv.at[n], to),
             to_dom(lists.at[to], got_lists.at[origin], isend.at[n], irecv.at[n], to),
         )
 
-    def ask(n, carry):
-        for copy in query_copies(n, ring.me):
+    def ask(n, to, source):
+        for copy in query_copies(n, to, ring.me):
             copy.start()
-        return carry
-
-    lax.fori_loop(0, ndom - 1, ask, 0)
+
+    for_peers(ndom, ring.me, ask)
     layer(
         True, me, nrep, fan, neigh_idx, nodes, table, stage, early, x_rows, weights1,
         chunks1, agg1, h_rows, h_cols, asend1, arecv1, hsend1, hrecv1, local1,
     )
     start_boundary(ring, send_idx, table, nodes, pick, outgoing, landing2, bsend2, brecv2)
 
-    def asked_by(n, carry):
-        for copy in query_copies(n, ring.source(n)):
+    def asked_by(n, to, source):
+        for copy in query_copies(n, to, source):
             copy.wait()
-        return carry
-
-    lax.fori_loop(0, ndom - 1, asked_by, 0)
+
+    for_peers(ndom, ring.me, asked_by)
     for copy in own_asked:
         copy.wait()
     into = pltpu.make_async_copy(got_lists, items, local.at[3 + len(blocks)])
@@ -364,13 +374,17 @@
                 partial[me, p, pl.ds(h, 1), :] = kept[:, h * LANE : (h + 1) * LANE]
         return carry
 
-    lax.fori_loop(0, ndom // together, score, 0)
+    steps = ndom // together // SHARES
+    share = steps * together
     copies = []
-    for step in range(nrep - 1):
-        copy = to_rep(partial.at[me], partial.at[me], psend.at[step], precv.at[step],
-                      lax.rem(me + 1 + step, nrep))
-        copy.start()
-        copies.append(copy)
+    for b in range(SHARES):
+        lax.fori_loop(b * steps, (b + 1) * steps, score, 0)
+        mine = partial.at[me, pl.ds(b * share, share)]
+        for step in range(nrep - 1):
+            copy = to_rep(mine, mine, psend.at[b, step], precv.at[b, step],
+                          lax.rem(me + 1 + step, nrep))
+            copy.start()
+            copies.append(copy)
     for copy in copies:
         copy.wait()
     added = partial[0]
@@ -379,18 +393,14 @@
     total[...] = added
     fetched[ring.me] = total[ring.me]
 
-    def answer(n, carry):
-        to = ring.target(n)
+    def answer(n, to, source):
         to_dom(total.at[to], fetched.at[ring.me], fsend.at[n], frecv.at[n], to).start()
-        return carry
-
-    def answered(n, carry):
-        to, source = ring.target(n), ring.source(n)
+
+    def answered(n, to, source):
         to_dom(total.at[to], fetched.at[source], fsend.at[n], frecv.at[n], to).wait()
-        return carry
-
-    lax.fori_loop(0, ndom - 1, answer, 0)
-    lax.fori_loop(0, ndom - 1, answered, 0)
+
+    for_peers(ndom, ring.me, answer)
+    for_peers(ndom, ring.me, answered)
 
     parts = []
     for h in range(half):
@@ -494,12 +504,12 @@
         + [dma(peers)] * 10
         + [dma(others)] * 2
         + [dma((4, nrep - 1))] * 2
-        + [dma(others)] * 2
+        + [dma((SHARES, nrep - 1))] * 2
         + per_layer
         + per_layer
         + [dma((9,))],
         compiler_params=pltpu.CompilerParams(
-            collective_id=1, has_side_effects=True, vmem_limit_bytes=56 * 1024 * 1024
+            collective_id=1, has_side_effects=True, vmem_limit_bytes=42 * 1024 * 1024
         ),
         name="graph_and_scores",
     )(*args)

time: 253 us -> 246 us (0.972)
  Pallas kernels: 243 us -> 239 us
    pallas_call x1, Pallas kernels: 243 us -> 239 us  [body(): pl.pallas_call(functools.partial(kernel, nrep, ndom, nx, nz, fan, nitems)...]
where the time goes in v5:
time: 246 us
  Pallas kernels  239 us (97%)
  local copies, waits for them, and re-layouts  3.66 us (1%)
    pallas_call x1, Pallas kernels, body(): pl.pallas_call(functools.partial(kernel, nrep, ndom, nx, nz, fan, nitems)...  239 us

profile of v5, /device:TPU:1, one launch (start us, length us, event | category | flops | bytes accessed | tf_op | source)
XLA Modules:
  0.0 245.6 jit_solution(8254823659161471005)
XLA Ops:
  0.6 0.7 copy.15
  1.3 0.0 copy-start.9
  1.3 0.0 copy-start.8
  1.3 0.0 copy-start.7
  1.3 0.6 fusion.5
  2.0 0.0 copy-done.9
  2.0 0.1 copy-done.8
  2.1 0.1 copy-done.7
  2.2 0.1 reshape.36.send_idx
  2.3 0.0 copy-start.6
  2.3 1.5 fusion.3
  3.8 0.0 copy-start
  3.8 0.0 copy-start.1
  3.8 0.0 copy-start.2
  3.8 0.0 copy-start.3
  3.8 0.0 copy-start.4
  3.8 0.0 copy-start.5
  3.9 0.0 copy-done.6
  3.9 0.1 reshape.39
  4.0 0.1 copy.13
  4.1 0.1 copy.14.lists
  4.2 0.7 copy-done
  4.9 0.0 copy-done.1
  4.9 0.0 copy-done.2
  5.0 0.0 copy-done.3
  5.0 0.0 copy-done.4
  5.0 0.0 copy-done.5
  5.0 239.0 %graph_and_scores.1 = (bf16[3072,128]{1,0:T(8,128)(2,1)S(1)}, f32[32,256]{1,0:T(8,128)S(1)}) custom-call(s32[30720]{0:T(1024)S(1)} %reshape.35.neigh_idx, s32[12288]{0:T(1024)S(1)} %reshape.36.send_idx, bf16[3072,128]{1,0:T(8,128)(2,1)S(1)} %copy-done, bf16[512,128]{1,0:T(8,128)(2,1)S(1)} %copy-done.1, bf16[512,128]{1,0:T(8,128)(2,1)S(1)} %copy-done.2, ...), custom_call_target="tpu_custom_call" | custom-call | tf_op jit(solution)/shard_map/graph_and_scores/pallas_call | solution.py:473
  244.1 0.9 copy.18
  244.9 0.6 copy.19
  (7 shorter events, 0.1 us)
Async XLA Ops:
  1.3 0.7 copy-start.9
  1.3 0.8 copy-start.8
  1.3 0.9 copy-start.7
  2.3 1.6 copy-start.6
  3.8 1.1 copy-start
  3.8 1.1 copy-start.1
  3.8 1.2 copy-start.2
  3.8 1.2 copy-start.3
  3.8 1.2 copy-start.4
  3.8 1.2 copy-start.5

commit v6 on v5

--- a/solution.py
+++ b/solution.py
@@ -112,10 +112,11 @@
 
 def start_boundary(ring, send_idx, table, nodes, pick, outgoing, landing, send, recv):
     count = pick.shape[0]
+    span = ring.ndom * count - 31
 
     def one(n, carry):
         to = ring.target(n)
-        pick_rows(lambda base, u: send_idx[to * count + base + u], table, pick, 32)
+        pick_rows(lambda base, u: send_idx.at[pl.ds(u, span)][to * count + base], table, pick, 32)
         outgoing[rows_of(to, count), :] = pick[...].astype(BF16)
         to_dom(
             outgoing.at[rows_of(to, count), :],
@@ -128,7 +129,7 @@
 
     lax.fori_loop(0, ring.ndom - 1, one, 0)
     me = ring.me
-    pick_rows(lambda base, u: send_idx[me * count + base + u], table, pick, 32)
+    pick_rows(lambda base, u: send_idx.at[pl.ds(u, span)][me * count + base], table, pick, 32)
     table[pl.ds(pl.multiple_of(nodes + me * count, 64), count), :] = pick[...]
 
 

time: 246 us -> 246 us (level)
  no operation moved by 1% of the time
where the time goes in v6:
time: 246 us
  Pallas kernels  239 us (97%)
  local copies, waits for them, and re-layouts  3.66 us (1%)
    pallas_call x1, Pallas kernels, body(): pl.pallas_call(functools.partial(kernel, nrep, ndom, nx, nz, fan, nitems)...  239 us

profile of v6, /device:TPU:1, one launch (start us, length us, event | category | flops | bytes accessed | tf_op | source)
XLA Modules:
  0.0 245.8 jit_solution(5293664194810942032)
XLA Ops:
  0.6 0.7 copy.15
  1.3 0.0 copy-start.9
  1.3 0.0 copy-start.8
  1.3 0.0 copy-start.7
  1.3 0.6 fusion.5
  2.0 0.0 copy-done.9
  2.0 0.1 copy-done.8
  2.1 0.1 copy-done.7
  2.2 0.1 reshape.36.send_idx
  2.3 0.0 copy-start.6
  2.3 1.5 fusion.3
  3.8 0.0 copy-start
  3.8 0.0 copy-start.1
  3.8 0.0 copy-start.2
  3.8 0.0 copy-start.3
  3.8 0.0 copy-start.4
  3.8 0.0 copy-start.5
  3.9 0.0 copy-done.6
  3.9 0.1 reshape.39
  4.0 0.1 copy.13
  4.1 0.1 copy.14.lists
  4.2 0.7 copy-done
  4.9 0.0 copy-done.1
  4.9 0.0 copy-done.2
  5.0 0.0 copy-done.3
  5.0 0.0 copy-done.4
  5.0 0.0 copy-done.5
  5.0 239.2 %graph_and_scores.1 = (bf16[3072,128]{1,0:T(8,128)(2,1)S(1)}, f32[32,256]{1,0:T(8,128)S(1)}) custom-call(s32[30720]{0:T(1024)S(1)} %reshape.35.neigh_idx, s32[12288]{0:T(1024)S(1)} %reshape.36.send_idx, bf16[3072,128]{1,0:T(8,128)(2,1)S(1)} %copy-done, bf16[512,128]{1,0:T(8,128)(2,1)S(1)} %copy-done.1, bf16[512,128]{1,0:T(8,128)(2,1)S(1)} %copy-done.2, ...), custom_call_target="tpu_custom_call" | custom-call | tf_op jit(solution)/shard_map/graph_and_scores/pallas_call | solution.py:474
  244.3 0.9 copy.18
  245.2 0.6 copy.19
  (7 shorter events, 0.1 us)
Async XLA Ops:
  1.3 0.7 copy-start.9
  1.3 0.8 copy-start.8
  1.3 0.9 copy-start.7
  2.3 1.6 copy-start.6
  3.8 1.1 copy-start
  3.8 1.1 copy-start.1
  3.8 1.2 copy-start.2
  3.8 1.2 copy-start.3
  3.8 1.2 copy-start.4
  3.8 1.2 copy-start.5
